TPU v7x, 512 devices: a whole 4x8x8 slice. The times are simulated.
512 devices in a mesh: dp: 32 (over z_lo, x, core), tensor: 16 (over y, z_hi).
Axes of the slice: x: 4, y: 8, z: 8 (z_hi: 2, z_lo: 4; z = z_hi * 4 + z_lo), core: 2. Of those that a mesh axis runs over, the one named last changes fastest.
Arguments:
- x_input: bfloat16 [8192, 4096], P('dp', 'tensor'), may hold values from -6 to 6
- z_input: bfloat16 [8192, 4096], P('dp', 'tensor'), may hold values from -8 to 8
- dt_raw: float32 [64, 8192], P('tensor', 'dp'), may hold values from -5 to 5
- b_rows: bfloat16 [8192, 128], P(('dp', 'tensor')), may hold values from -2 to 2
- c_rows: bfloat16 [8192, 128], P(('dp', 'tensor')), may hold values from -2 to 2
- a_log: float32 [64], P('tensor'), may hold values from -4 to 1
- skip_gain: float32 [64], P('tensor'), may hold values from 0.5 to 2
- dt_bias: float32 [64], P('tensor'), may hold values from -3 to 0
- norm_gain: float32 [4096], P('tensor'), may hold values from 0.5 to 1.5
- w_out: bfloat16 [4096, 2048], P('tensor'), may hold values from -0.09375 to 0.09375
- grad_rows: bfloat16 [8192, 2048], P(('dp', 'tensor')), may hold values from -6 to 6
- doc_ids: int32 [8192], P('dp'), may hold values from 0 to 255, never falling along the last dimension, each value on 1 to 64 neighbouring positions
Outputs:
- grad_x: bfloat16 [8192, 4096], P('dp', 'tensor')
- grad_z: bfloat16 [8192, 4096], P('dp', 'tensor')
- grad_dt: float32 [64, 8192], P('tensor', 'dp')
- grad_b: float32 [8192, 128], P(('dp', 'tensor'))
- grad_c: float32 [8192, 128], P(('dp', 'tensor'))
- grad_w_out: bfloat16 [4096, 2048], P('tensor')
- grad_norm: float32 [4096], P('tensor')
- grad_a_log: float32 [64], P('tensor')
- grad_skip: float32 [64], P('tensor')
- grad_dt_bias: float32 [64], P('tensor')
Inputs may be any that keep to these rules, and one draw needn't show every extreme that they name: `doc_ids`: ids never fall along the tokens; a document has at most 64 tokens.
All inputs are finite; a program needn't handle non-finite values.
Results may differ from a plain program's by a relative error of at most 0.025.
Values may be sent and summed in bfloat16 or wider, within the bound.
A program may use at most 64 MiB of HBM per device.

v0:
```python
import jax
import jax.numpy as jnp
from jax import lax
from jax.sharding import PartitionSpec as P

SPAN = 128


epsilon = 1e-05
exact = lax.Precision.HIGHEST


def ssd_gate(x_all, z_all, dt_raw, b_all, c_all, a_log, skip_gain, dt_bias, doc_ids, span):
    seqlen = x_all.shape[0]
    nheads = dt_raw.shape[0]
    head_size = x_all.shape[1] // nheads
    blocks = seqlen // span
    low = jnp.bfloat16
    wide = jnp.float32
    step_size = jax.nn.softplus(dt_raw + dt_bias[:, None])
    log_decay = -jnp.exp(a_log)[:, None] * step_size
    cum_decay = jnp.cumsum(log_decay.reshape(nheads, blocks, span), axis=2)
    seg_blocks = doc_ids.reshape(blocks, span)
    prev_seg = jnp.concatenate([jnp.full((1,), -1, jnp.int32), seg_blocks[:-1, -1]])
    causal = jnp.arange(span)[:, None] >= jnp.arange(span)[None, :]
    same_doc = (causal[None] & (seg_blocks[:, :, None] == seg_blocks[:, None, :])).astype(
        jnp.float32
    )
    log_gap = cum_decay[:, :, :, None] - cum_decay[:, :, None, :]
    decay_in = jnp.exp(jnp.minimum(log_gap, 0.0)) * same_doc[None]
    step_blocks = step_size.reshape(nheads, blocks, span)
    x_heads = x_all.reshape(blocks, span, nheads, head_size)
    x_low = x_heads.astype(low)
    b_low = b_all.reshape(blocks, span, -1).astype(low)
    c_low = c_all.reshape(blocks, span, -1).astype(low)
    scores = jnp.einsum("cin,cjn->cij", c_low, b_low, preferred_element_type=wide, precision=exact)
    mixing = decay_in * scores[None] * step_blocks[:, :, None, :]
    y_intra = jnp.einsum(
        "hcij,cjhp->cihp", mixing.astype(low), x_low, preferred_element_type=wide, precision=exact
    )
    end_mask = (seg_blocks[:, -1:] == seg_blocks).astype(jnp.float32)
    to_end = jnp.exp(cum_decay[:, :, -1:] - cum_decay) * end_mask[None] * step_blocks
    weighted = x_heads * to_end.transpose(1, 2, 0)[:, :, :, None]
    states = jnp.einsum(
        "cjhp,cjn->chpn", weighted.astype(low), b_low, preferred_element_type=wide, precision=exact
    )
    carry_mask = (seg_blocks[:, -1] == prev_seg).astype(jnp.float32)
    carry_decay = jnp.exp(cum_decay[:, :, -1]) * carry_mask[None]

    def advance(state, inputs):
        block_state, block_decay = inputs
        return (block_decay[:, None, None] * state + block_state, state)

    _, entering = lax.scan(
        advance, jnp.zeros(states.shape[1:], jnp.float32), (states, carry_decay.T)
    )
    start_mask = (seg_blocks == prev_seg[:, None]).astype(jnp.float32)
    from_start = jnp.exp(cum_decay) * start_mask[None]
    y_inter = (
        jnp.einsum(
            "cin,chpn->cihp",
            c_low,
            entering.astype(low),
            preferred_element_type=wide,
            precision=exact,
        )
        * from_start.transpose(1, 2, 0)[:, :, :, None]
    )
    outputs = y_intra + y_inter + skip_gain[None, None, :, None] * x_heads
    gate_in = z_all.reshape(blocks, span, nheads, head_size)
    gated = outputs * jax.nn.silu(gate_in)
    return gated.reshape(seqlen, nheads * head_size)


def per_device(
    x_input,
    z_input,
    dt_raw,
    b_rows,
    c_rows,
    a_log,
    skip_gain,
    dt_bias,
    norm_gain,
    w_out,
    grad_rows,
    doc_ids,
):
    b_full, c_full = (
        lax.all_gather(b_rows, "tensor", axis=0, tiled=True),
        lax.all_gather(c_rows, "tensor", axis=0, tiled=True),
    )

    def core(x_all, z_all, dt_all, b_all, c_all, a_all, skip_all, bias_all):
        return ssd_gate(
            x_all, z_all, dt_all, b_all, c_all, a_all, skip_all, bias_all, doc_ids, SPAN
        )

    gated, pull = jax.vjp(
        core,
        x_input.astype(jnp.float32),
        z_input.astype(jnp.float32),
        dt_raw,
        b_full.astype(jnp.float32),
        c_full.astype(jnp.float32),
        a_log,
        skip_gain,
        dt_bias,
    )
    local_channels = gated.shape[1]
    channels = local_channels * lax.axis_size("tensor")
    sum_squares = lax.psum(jnp.sum(gated * gated, axis=1), "tensor")
    inv_rms = lax.rsqrt(sum_squares / channels + epsilon)
    normed = (gated * inv_rms[:, None] * norm_gain).astype(jnp.bfloat16)
    piece = lax.all_gather(grad_rows, "tensor", axis=0, tiled=True)
    weight_acc = jnp.dot(normed.T, piece, preferred_element_type=jnp.float32)
    mixed = jnp.dot(piece, w_out.T, preferred_element_type=jnp.float32)
    slope_sum = lax.psum(jnp.sum(gated * norm_gain * mixed, axis=1), "tensor")
    norm_grad = jnp.sum(mixed * gated * inv_rms[:, None], axis=0)
    cube = inv_rms * inv_rms * inv_rms
    grad_gated = (
        inv_rms[:, None] * norm_gain * mixed - gated * (cube * (slope_sum / channels))[:, None]
    )
    grad_xf, grad_zf, grad_dt, grad_bf, grad_cf, grad_al, grad_sk, grad_db = pull(grad_gated)
    grad_b, grad_c = (
        lax.psum_scatter(grad_bf, "tensor", scatter_dimension=0, tiled=True),
        lax.psum_scatter(grad_cf, "tensor", scatter_dimension=0, tiled=True),
    )
    weight_total, norm_total, al_total, sk_total, db_total = lax.psum(
        (weight_acc, norm_grad, grad_al, grad_sk, grad_db), "dp"
    )
    grad_w_out = weight_total.astype(jnp.bfloat16)
    return (
        grad_xf.astype(jnp.bfloat16),
        grad_zf.astype(jnp.bfloat16),
        grad_dt,
        grad_b,
        grad_c,
        grad_w_out,
        norm_total,
        al_total,
        sk_total,
        db_total,
    )


def solution(mesh):
    in_specs = (
        P("dp", "tensor"),
        P("dp", "tensor"),
        P("tensor", "dp"),
        P(("dp", "tensor"), None),
        P(("dp", "tensor"), None),
        P("tensor"),
        P("tensor"),
        P("tensor"),
        P("tensor"),
        P("tensor", None),
        P(("dp", "tensor"), None),
        P("dp"),
    )
    out_specs = (
        P("dp", "tensor"),
        P("dp", "tensor"),
        P("tensor", "dp"),
        P(("dp", "tensor"), None),
        P(("dp", "tensor"), None),
        P("tensor", None),
        P("tensor"),
        P("tensor"),
        P("tensor"),
        P("tensor"),
    )
    return jax.shard_map(
        per_device, mesh=mesh, in_specs=in_specs, out_specs=out_specs, check_vma=False
    )
```

profile of v0, /device:TPU:1, one launch (start us, length us, event | category | flops | bytes accessed | tf_op | source)
XLA Modules:
  0.0 674.0 jit_solution(7682512521189007579)
XLA Ops:
  8.0 1.3 slice.13
  11.6 1.2 reduce_window_sum.22
  16.0 51.3 %all_gather.10 = bf16[256,128]{1,0:T(8,128)(2,1)S(1)} all-gather(bf16[16,128]{1,0:T(8,128)(2,1)} %param.19), channel_id=1, replica_groups=mesh['dp'=32,'tensor'=16] {'tensor'}, dimensions={0}, use_global_device_ids=true | all-gather | bytes 69632 | tf_op jit(solution)/shard_map/all_gather | solution.py:90
  67.2 41.6 %all_gather.9 = bf16[256,128]{1,0:T(8,128)(2,1)S(1)} all-gather(bf16[16,128]{1,0:T(8,128)(2,1)} %param.20), channel_id=1, replica_groups=mesh['dp'=32,'tensor'=16] {'tensor'}, dimensions={0}, use_global_device_ids=true | all-gather | bytes 69632 | tf_op jit(solution)/shard_map/all_gather | solution.py:91
  109.8 1.1 copy.142
  111.1 1.2 reshape.214
  113.5 1.7 multiply_reduce_fusion.5
  115.8 45.0 %psum.49 = f32[256]{0:T(256)S(1)} all-reduce(f32[256]{0:T(256)} %bitcast.183), channel_id=1, replica_groups=mesh['dp'=32,'tensor'=16] {'tensor'}, use_global_device_ids=true, to_apply=%region_4.5 | all-reduce | flops 256 | bytes 2048 | tf_op jit(solution)/shard_map/psum | solution.py:112
  160.9 2.3 multiply_reduce_fusion.1
  163.2 39.5 %psum.50 = f32[256]{0:T(256)S(1)} all-reduce(f32[256]{0:T(256)S(1)} %get-tuple-element.279), channel_id=1, replica_groups=mesh['dp'=32,'tensor'=16] {'tensor'}, use_global_device_ids=true, to_apply=%region_6.7 | all-reduce | flops 256 | bytes 2048 | tf_op jit(solution)/shard_map/psum | solution.py:118
  202.7 1.6 multiply_reduce_fusion
  204.8 1.9 multiply_reduce_fusion.2
  206.6 2.1 fusion.70
  210.4 1.0 multiply_reduce_fusion.3
  213.2 5.0 reduce_window_sum.23
  218.3 1.3 fusion.71
  219.6 1.8 fusion.37
  221.4 1.2 negate_multiply_fusion
  224.6 178.4 %all-reduce.4 = (bf16[256,2048]{1,0:T(8,128)(2,1)}, f32[256]{0:T(256)}, f32[4]{0:T(128)}, f32[4]{0:T(128)}, f32[4]{0:T(128)}) all-reduce(f32[256,2048]{1,0:T(8,128)S(1)} %fusion.37, f32[256]{0:T(256)} %get-tuple-element.278, f32[4]{0:T(128)} %negate_multiply_fusion, f32[4]{0:T(128)} %reduce_sum.195, ...), channel_id=1, replica_groups=mesh['dp'=32,'tensor'=16] {'dp'}, use_global_device_ids=true, to_apply=%region_20.21 | all-reduce | flops 524556 | bytes 3147872 | tf_op jit(solution)/shard_map/psum | solution.py:129
  403.1 1.6 fusion.10
  404.9 0.9 reshape.212
  405.9 0.9 reshape.213
  406.8 42.7 %reduce-scatter.5.cloned.1.call-done = f32[16,128]{1,0:T(8,128)} async-done(((f32[256,128]{1,0:T(8,128)}), f32[16,128]{1,0:T(8,128)}) %reduce-scatter.5.cloned.1.call-update) | async-done | bytes 8208 | tf_op jit(solution)/shard_map/reduce_scatter | solution.py:127
  449.5 218.0 %reduce-scatter.3.cloned.1.call-done = f32[16,128]{1,0:T(8,128)} async-done(((f32[256,128]{1,0:T(8,128)}), f32[16,128]{1,0:T(8,128)}) %reduce-scatter.3.cloned.1.call-update) | async-done | bytes 8208 | tf_op jit(solution)/shard_map/reduce_scatter | solution.py:126
  (139 shorter events, 15.8 us)
Async XLA Ops:
  7.2 153.7 %copy-start = (bf16[256,2048]{1,0:T(8,128)(2,1)S(1)}, bf16[256,2048]{1,0:T(8,128)(2,1)}, u32[]{:S(2)}) copy-start(bf16[256,2048]{1,0:T(8,128)(2,1)} %param.25) | copy-start | bytes 3145732
  7.2 153.7 %all-gather.2.cloned.1.call-start = ((), (), s32[]{:S(2)}) async-start(), calls=%async_computation.2 | async-start | bytes 1114112 | tf_op jit(solution)/shard_map/all_gather | solution.py:115
  7.9 441.6 %reduce-scatter.5.cloned.1.call-start = ((), (), s32[]{:S(2)}) async-start(), calls=%async_computation.4 | async-start | bytes 139264 | tf_op jit(solution)/shard_map/reduce_scatter | solution.py:127
  12.8 100.6 %copy-start.23 = (f32[4,2,128]{2,0,1:T(4,128)}, f32[4,2,128]{2,0,1:T(4,128)S(1)}, u32[]{:S(2)}) copy-start(f32[4,2,128]{2,0,1:T(4,128)S(1)} %copy.139) | copy-start | bytes 12292
  15.1 97.7 %copy-start.17 = (f32[2,128]{1,0:T(2,128)}, f32[2,128]{1,0:T(2,128)S(1)}, u32[]{:S(2)}) copy-start(f32[2,128]{1,0:T(2,128)S(1)} %get-tuple-element.330) | copy-start | bytes 3076
  15.1 97.8 %copy-start.19 = (f32[2,128]{1,0:T(2,128)}, f32[2,128]{1,0:T(2,128)S(1)}, u32[]{:S(2)}) copy-start(f32[2,128]{1,0:T(2,128)S(1)} %get-tuple-element.331) | copy-start | bytes 3076
  15.2 97.6 %copy-start.14 = (f32[4,2,1]{0,1,2:T(2,128)}, f32[4,2,1]{0,1,2:T(2,128)S(1)}, u32[]{:S(2)}) copy-start(f32[4,2,1]{0,1,2:T(2,128)S(1)} %copy.144) | copy-start | bytes 100
  109.7 3.7 copy-start.7
  111.1 2.4 copy-start.6
  115.2 87.5 %copy-start.4 = (bf16[256,256]{1,0:T(8,128)(2,1)S(1)}, bf16[256,256]{1,0:T(8,128)(2,1)}, u32[]{:S(2)}) copy-start(bf16[256,256]{1,0:T(8,128)(2,1)} %param.16) | copy-start | bytes 393220
  160.8 43.5 %copy-start.13 = (f32[256]{0:T(256)}, f32[256]{0:T(256)S(1)}, u32[]{:S(2)}) copy-start(f32[256]{0:T(256)S(1)} %add_rsqrt_fusion) | copy-start | bytes 3076
  206.6 2.9 copy-start.1
  206.6 2.9 copy-start.30
  210.0 2.8 copy-start.10
  210.0 2.8 copy-start.12
  210.0 2.8 copy-start.20
  210.0 3.1 copy-start.18
  210.0 8.2 %copy-start.16 = (f32[4,256]{1,0:T(4,128)S(1)}, f32[4,256]{1,0:T(4,128)}, u32[]{:S(2)}) copy-start(f32[4,256]{1,0:T(4,128)} %param.18) | copy-start | bytes 12292
  210.0 8.2 %copy-start.25 = (f32[4]{0:T(128)S(1)}, f32[4]{0:T(128)}, u32[]{:S(2)}) copy-start(f32[4]{0:T(128)} %param.23) | copy-start | bytes 52
  210.0 8.2 %copy-start.27 = (f32[4]{0:T(128)S(1)}, f32[4]{0:T(128)}, u32[]{:S(2)}) copy-start(f32[4]{0:T(128)} %copy-done.26) | copy-start | bytes 52
  212.3 455.2 %reduce-scatter.3.cloned.1.call-start = ((), (), s32[]{:S(2)}) async-start(), calls=%async_computation.3 | async-start | bytes 139264 | tf_op jit(solution)/shard_map/reduce_scatter | solution.py:126
  219.6 183.5 %copy-start.24 = (f32[4,2,128]{2,0,1:T(4,128)S(1)}, f32[4,2,128]{2,0,1:T(4,128)}, u32[]{:S(2)}) copy-start(f32[4,2,128]{2,0,1:T(4,128)} %copy-done.23) | copy-start | bytes 12292
  221.3 181.7 %copy-start.2 = (f32[2,128,4,64]{1,3,2,0:T(8,128)S(1)}, f32[2,128,4,64]{1,3,2,0:T(8,128)}, u32[]{:S(2)}) copy-start(f32[2,128,4,64]{1,3,2,0:T(8,128)} %copy-done.1) | copy-start | bytes 786436
  224.6 181.1 %copy-start.5 = (bf16[2,128,4,64]{1,3,2,0:T(8,128)(2,1)S(1)}, bf16[2,128,4,64]{1,3,2,0:T(8,128)(2,1)}, u32[]{:S(2)}) copy-start(bf16[2,128,4,64]{1,3,2,0:T(8,128)(2,1)} %get-tuple-element.325) | copy-start | bytes 393220
  (10 other events, 14.6 us)
Sparse Core Ops, SparseCore 0:
  11.2 95.9 all-gather.1
  212.4 237.1 reduce-scatter.4
  455.2 212.2 reduce-scatter.2
where the time goes:
time: 679 us; the launch traced here: 674 us
  blocking collectives  356 us (52%)
  waiting for transfers between devices  261 us (38%)
  other arithmetic  19.8 us (3%)
  between operations  14.3 us (2%)
  matrix products  12.5 us (2%)
  local copies, waits for them, and re-layouts  9.94 us (1%)
    reduce_scatter x1, waiting for transfers between devices, per_device(): lax.psum_scatter(grad_bf, 'tensor', scatter_dimension=0, tiled=True)  218 us
    psum x1, blocking collectives, per_device(): lax.psum((weight_acc, norm_grad, grad_al, grad_sk, grad_db), 'dp')  178 us
    all_gather x1, blocking collectives, per_device(): lax.all_gather(b_rows, 'tensor', axis=0, tiled=True)  51.3 us
    psum x1, blocking collectives, per_device(): sum_squares = lax.psum(jnp.sum(gated * gated, axis=1), 'tensor')  45 us
    reduce_scatter x1, waiting for transfers between devices, per_device(): lax.psum_scatter(grad_cf, 'tensor', scatter_dimension=0, tiled=True)  42.7 us
    all_gather x1, blocking collectives, per_device(): lax.all_gather(c_rows, 'tensor', axis=0, tiled=True)  41.6 us
    psum x1, blocking collectives, per_device(): slope_sum = lax.psum(jnp.sum(gated * norm_gain * mixed, axis=1), 'tensor')  39.5 us
  transfers between devices with their start and end apart: 3, of which 2 were waited for; matrix products, arithmetic and copies ran while one was open for 4% of the time, Pallas kernels for 0%

commit v1 on v0

v1 whole, which is shorter than its diff:
```python
import jax
import jax.numpy as jnp
from jax import lax
from jax.experimental import pallas as pl
from jax.experimental.pallas import tpu as pltpu
from jax.sharding import PartitionSpec as P

MESH = pl.DeviceIdType.MESH
HI = lax.Precision.HIGHEST
F32 = jnp.float32
BF16 = jnp.bfloat16
EPS = 1e-05

T = 256
C = 256
HD = 64
NH = 4
N = 128
DW = 2048
NT = 16
NY = 8
CHUNKS = 4
CW = DW // CHUNKS
INNER = C * NT


def nn(a, b, prec=None):
    return lax.dot_general(a, b, (((1,), (0,)), ((), ())), precision=prec, preferred_element_type=F32)


def nt(a, b, prec=None):
    return lax.dot_general(a, b, (((1,), (1,)), ((), ())), precision=prec, preferred_element_type=F32)


def tn(a, b, prec=None):
    return lax.dot_general(a, b, (((0,), (0,)), ((), ())), precision=prec, preferred_element_type=F32)


def kernel(
    x_ref, z_ref, dt_ref, b_ref, c_ref, al_ref, sk_ref, db_ref, gain_ref, w_ref, g_ref, ids_ref,
    gx_ref, gz_ref, gdt_ref, gb_ref, gc_ref, gw_ref, gn_ref, gs_ref,
    bc, gall, st1, st2, wk, r1, s2, r2, s3, r3, dbc, dbr, pk, p1, p2, p2r, p3, p3r,
    rw, pr, mb, tge, xt, xtb, silt, dst, yt, gt, ks, hs, qs, ws, dxt, nrm, mx,
    bc_s, bc_r, g_s, g_r, st1_s, st1_r, st2_s, st2_r, c_s, c_r, x_s, x_r, z_s, z_r,
    az_s, az_r, ax_s, ax_r, ac_s, ac_r, db_s, db_r, p_s, p_r,
):
    dp = lax.axis_index("dp")
    me = lax.axis_index("tensor")
    zl, xi, core = dp // 8, (dp // 2) % 4, dp % 2
    y, zh = me // 2, me % 2

    def at_x(o):
        return zl * 8 + ((xi + o) % 4) * 2 + core

    def at_z(o):
        return ((zl + o) % 4) * 8 + xi * 2 + core

    other_core = zl * 8 + xi * 2 + (1 - core)
    dp_peers = [other_core] + [at_x(o) for o in (1, 2, 3)] + [at_z(o) for o in (1, 2, 3)]

    barrier = pltpu.get_barrier_semaphore()
    for o in range(1, NT):
        pl.semaphore_signal(barrier, inc=1, device_id=(dp, (me + o) % NT), device_id_type=MESH)
    for peer in dp_peers:
        pl.semaphore_signal(barrier, inc=1, device_id=(peer, me), device_id_type=MESH)

    started = []

    def send(src, dst, ss, rs, dev):
        copy = pltpu.make_async_remote_copy(
            src_ref=src, dst_ref=dst, send_sem=ss, recv_sem=rs, device_id=dev, device_id_type=MESH
        )
        copy.start()
        started.append(copy)
        return copy

    def rows(i, n):
        return pl.ds(pl.multiple_of(i * n, n), n)

    bc[rows(me, 16), 0:N] = b_ref[...]
    bc[rows(me, 16), N:2 * N] = c_ref[...]
    gall[rows(me, 16), :] = g_ref[...]

    pl.semaphore_wait(barrier, NT - 1 + len(dp_peers))

    bc_copies = []
    for o in range(1, NT):
        mine = bc.at[rows(me, 16), :]
        bc_copies.append(send(mine, mine, bc_s.at[o - 1], bc_r.at[o - 1], (dp, (me + o) % NT)))

    def piece(slot):
        return gall.at[rows(slot, 16), :]

    ring = {}

    def hop(direction, kind, k):
        ysrc = (y - direction * k + NY) % NY
        slot = ysrc * 2 + (zh if kind == 0 else 1 - zh)
        to = ((y + direction + NY) % NY) * 2 + zh
        i = 1 + ((0 if direction > 0 else 1) * 2 + kind) * 4 + k
        ring[direction, kind, k + 1] = send(piece(slot), piece(slot), g_s.at[i], g_r.at[i], (dp, to))

    zcopy = send(piece(me), piece(me), g_s.at[0], g_r.at[0], (dp, y * 2 + 1 - zh))
    hop(1, 0, 0)
    hop(-1, 0, 0)

    def last_hop(direction, kind):
        return 4 if (direction > 0) == (kind == 0) else 3

    def ring_partner():
        zcopy.wait_recv()
        hop(1, 1, 0)
        hop(-1, 1, 0)

    def ring_level(k):
        for kind in (0, 1):
            for direction in (1, -1):
                if k <= last_hop(direction, kind):
                    ring[direction, kind, k].wait_recv()
                    if k < last_hop(direction, kind):
                        hop(direction, kind, k)

    hrow = lax.broadcasted_iota(jnp.int32, (NH, T), 0)

    def per_head(ref):
        v = jnp.full((NH, T), ref[0], F32)
        for h in range(1, NH):
            v = jnp.where(hrow == h, ref[h], v)
        return v

    pre = dt_ref[...] + per_head(db_ref)
    step = jnp.maximum(pre, 0.0) + jnp.log1p(jnp.exp(-jnp.abs(pre)))
    sig = 1.0 / (1.0 + jnp.exp(-pre))
    ea = jnp.exp(per_head(al_ref))
    ld = -ea * step
    rw[...] = jnp.zeros_like(rw)
    rw[0:NH, :] = step
    rw[4:5, :] = ids_ref[...].astype(F32)
    rw[5:6, :] = gain_ref[...]
    rw[8:8 + NH, :] = ld
    ri = lax.broadcasted_iota(jnp.int32, (T, T), 0)
    ci = lax.broadcasted_iota(jnp.int32, (T, T), 1)
    tril = jnp.where(ri >= ci, 1.0, 0.0)
    eye = jnp.where(ri == ci, 1.0, 0.0)
    tge[...] = tril.astype(BF16)
    cols = nt(eye, rw[0:8, :], HI)
    cumc = nt(tril, rw[8:16, :], HI)
    cumr = nt(rw[8:16, :], tril, HI)
    idr = rw[4:5, :]
    mb[...] = jnp.where((ri <= ci) & (cols[:, 4:5] == idr), 0.0, -1e30)
    gain_col = cols[:, 5:6]

    ring_partner()

    xv = x_ref[...].astype(F32).T
    xt[...] = xv
    xtb[...] = xv.astype(BF16)
    zv = z_ref[...].astype(F32).T
    sg = 1.0 / (1.0 + jnp.exp(-zv))
    silt[...] = zv * sg
    dst[...] = sg * (1.0 + zv * (1.0 - sg))

    ks[...] = jnp.zeros_like(ks)
    hs[...] = jnp.zeros_like(hs)

    for copy in bc_copies:
        copy.wait_recv()
    ring_level(1)
    ball = bc[:, 0:N]
    call = bc[:, N:2 * N]
    scores = nt(ball, call)
    mx[...] = scores
    for h in range(NH):
        for s0 in range(0, T, 64):
            t0 = 0 if s0 < 128 else 128
            gap = cumr[h:h + 1, t0:] - cumc[s0:s0 + 64, h:h + 1] + mb[s0:s0 + 64, t0:]
            w = jnp.exp(gap) * cols[s0:s0 + 64, h:h + 1]
            hs[h, s0:s0 + 64, t0:] = w.astype(BF16)
            ks[h, s0:s0 + 64, t0:] = (w * mx[s0:s0 + 64, t0:]).astype(BF16)
        c0 = h * HD
        yv = nn(xtb[c0:c0 + HD, :], ks[h]) + sk_ref[h] * xt[c0:c0 + HD, :]
        yt[c0:c0 + HD, :] = yv
        gt[c0:c0 + HD, :] = yv * silt[c0:c0 + HD, :]
        if h == 1:
            ring_level(2)

    def all_stats(st, row, ss, rs):
        st[me, 0:1, :] = row[:, 0:128]
        st[me, 1:2, :] = row[:, 128:256]
        return [
            send(st.at[me], st.at[me], ss.at[o - 1], rs.at[o - 1], (dp, (me + o) % NT))
            for o in range(1, NT)
        ]

    def sum_stats(st, copies):
        for copy in copies:
            copy.wait_recv()
        tot = jnp.sum(st[...], axis=0)
        return jnp.concatenate([tot[0:1, :], tot[1:2, :]], axis=1)

    gated = gt[...]
    stat1 = all_stats(st1, jnp.sum(gated * gated, axis=0, keepdims=True), st1_s, st1_r)
    ring_level(3)
    inv = lax.rsqrt(sum_stats(st1, stat1) / INNER + EPS)
    nrm[...] = (gt[...] * inv * gain_col).astype(BF16)
    ring_level(4)

    core_copies = []
    for k in range(CHUNKS):
        wk[k] = nn(nrm[...], gall[:, k * CW:(k + 1) * CW]).astype(BF16)
        core_copies.append(
            send(wk.at[k, rows(1 - core, 128), :], r1.at[k], c_s.at[k], c_r.at[k], (other_core, me))
        )

    mixed = nt(w_ref[...], gall[...])
    mx[...] = mixed
    stat2 = all_stats(
        st2, jnp.sum(gt[...] * gain_col * mixed, axis=0, keepdims=True), st2_s, st2_r
    )

    x_copies = []

    def stage_x(k):
        core_copies[k].wait_recv()
        s2[k] = (wk[k, rows(core, 128), :].astype(F32) + r1[k].astype(F32)).astype(BF16)
        x_copies.append([
            send(
                s2.at[k, rows((xi + o) % 4, 32), :], r2.at[k, o - 1],
                x_s.at[k * 3 + o - 1], x_r.at[k * 3 + o - 1], (at_x(o), me),
            )
            for o in (1, 2, 3)
        ])

    z_copies = []

    def stage_z(k):
        for copy in x_copies[k]:
            copy.wait_recv()
        tot = s2[k, rows(xi, 32), :].astype(F32)
        for o in range(3):
            tot = tot + r2[k, o].astype(F32)
        tot = tot.astype(BF16)
        for q in range(4):
            s3[k, q] = tot[:, q * 128:(q + 1) * 128]
        z_copies.append([
            send(
                s3.at[k, (zl + o) % 4], r3.at[k, o - 1],
                z_s.at[k * 3 + o - 1], z_r.at[k * 3 + o - 1], (at_z(o), me),
            )
            for o in (1, 2, 3)
        ])

    az_copies, ax_copies, ac_copies = [], [], []

    def gather_z(k):
        for copy in z_copies[k]:
            copy.wait_recv()
        tot = s3[k, zl].astype(F32)
        for o in range(3):
            tot = tot + r3[k, o].astype(F32)
        r0 = rows(core * 4 + xi, 32)
        col = pl.ds(pl.multiple_of(k * CW + zl * 128, 128), 128)
        gw_ref[r0, col] = tot.astype(BF16)
        az_copies.append([
            send(
                gw_ref.at[r0, col], gw_ref.at[r0, col],
                az_s.at[k * 3 + o - 1], az_r.at[k * 3 + o - 1], (at_z(o), me),
            )
            for o in (1, 2, 3)
        ])

    def gather_x(k):
        for copy in az_copies[k]:
            copy.wait_recv()
        block = gw_ref.at[rows(core * 4 + xi, 32), k * CW:(k + 1) * CW]
        ax_copies.append([
            send(block, block, ax_s.at[k * 3 + o - 1], ax_r.at[k * 3 + o - 1], (at_x(o), me))
            for o in (1, 2, 3)
        ])

    def gather_core(k):
        for copy in ax_copies[k]:
            copy.wait_recv()
        block = gw_ref.at[rows(core, 128), k * CW:(k + 1) * CW]
        ac_copies.append(send(block, block, ac_s.at[k], ac_r.at[k], (other_core, me)))

    for k in range(CHUNKS):
        stage_x(k)

    slope = sum_stats(st2, stat2) / INNER
    mixed = mx[...]
    gated = gt[...]
    ng = nt(jnp.ones((8, T), F32), mixed * gated * inv, HI)
    ggt = gain_col * mixed * inv - gated * (inv * inv * inv * slope)
    gz_ref[...] = (ggt * yt[...] * dst[...]).T.astype(BF16)
    yt[...] = ggt * silt[...]

    ws[...] = jnp.zeros_like(ws)
    qs[...] = jnp.zeros_like(qs)
    pr[...] = jnp.zeros_like(pr)
    strict = jnp.where(ri < ci, 1.0, 0.0)

    def back(h):
        c0 = h * HD
        dy = yt[c0:c0 + HD, :]
        xh = xt[c0:c0 + HD, :]
        dyb = dy.astype(BF16)
        for s0, t0 in ((0, 0), (128, 128)):
            dm = tn(xtb[c0:c0 + HD, s0:s0 + 128], dyb[:, t0:])
            qs[s0:s0 + 128, t0:] = (dm * ks[h, s0:s0 + 128, t0:].astype(F32)).astype(BF16)
            ws[s0:s0 + 128, t0:] += dm * hs[h, s0:s0 + 128, t0:].astype(F32)
        top = jnp.sum(nn(qs[0:128, :], tge[...]) * strict[0:128, :], axis=0, keepdims=True)
        low = jnp.sum(
            nn(qs[128:, 128:], tge[128:, 128:]) * strict[128:, 128:], axis=0, keepdims=True
        )
        dld = jnp.concatenate([top[:, 0:128], top[:, 128:] + low], axis=1)
        dxi = nt(dyb, ks[h])
        direct = jnp.sum(xh * dxi, axis=0, keepdims=True) / rw[h:h + 1, :]
        dxt[c0:c0 + HD, :] = dxi + sk_ref[h] * dy
        pr[h:h + 1, :] = jnp.sum(dy * xh, axis=0, keepdims=True)
        pr[4 + h:5 + h, :] = dld
        pr[8 + h:9 + h, :] = direct

    for h in range(NH):
        back(h)
        stage_z(h)

    dld = pr[4:8, :]
    ddt = (pr[8:12, :] - ea * dld) * sig
    gdt_ref[...] = ddt
    pr[4:8, :] = dld * ld
    pr[8:12, :] = ddt

    wb = ws[...].astype(BF16)
    dbc[:, 0:N] = nn(wb, call).astype(BF16)
    dbc[:, N:2 * N] = tn(wb, ball).astype(BF16)
    d_copies = [
        send(
            dbc.at[rows((me + o) % NT, 16), :], dbr.at[o - 1],
            db_s.at[o - 1], db_r.at[o - 1], (dp, (me + o) % NT),
        )
        for o in range(1, NT)
    ]

    small = nt(jnp.ones((8, T), F32), pr[...], HI)
    pk[...] = jnp.zeros_like(pk)
    pk[0:1, :] = ng[0:1, 0:128]
    pk[1:2, :] = ng[0:1, 128:256]
    pk[2:3, 0:16] = small[0:1, :]
    pc = send(pk, p1, p_s.at[0], p_r.at[0], (other_core, me))

    for k in range(CHUNKS):
        gather_z(k)

    pc.wait_recv()
    p2[...] = pk[...] + p1[...]
    px = [
        send(p2, p2r.at[o - 1], p_s.at[o], p_r.at[o], (at_x(o), me)) for o in (1, 2, 3)
    ]

    for k in range(CHUNKS):
        gather_x(k)

    gx_ref[...] = dxt[...].T.astype(BF16)
    for copy in px:
        copy.wait_recv()
    p3[...] = p2[...] + p2r[0] + p2r[1] + p2r[2]
    pz = [
        send(p3, p3r.at[o - 1], p_s.at[o + 3], p_r.at[o + 3], (at_z(o), me)) for o in (1, 2, 3)
    ]

    for copy in d_copies:
        copy.wait_recv()
    tot = dbc[rows(me, 16), :].astype(F32)
    for o in range(NT - 1):
        tot = tot + dbr[o].astype(F32)
    gb_ref[...] = tot[:, 0:N]
    gc_ref[...] = tot[:, N:2 * N]

    for k in range(CHUNKS):
        gather_core(k)

    for copy in pz:
        copy.wait_recv()
    tot = p3[...] + p3r[0] + p3r[1] + p3r[2]
    gn_ref[...] = tot[0:2, :]
    gs_ref[...] = tot[2:3, :]

    for copy in ac_copies:
        copy.wait_recv()
    for copy in started:
        copy.wait_send()


def per_device(x, z, dt, b, c, a_log, skip, bias, gain, w, g, ids):
    vmem = pl.BlockSpec(memory_space=pltpu.VMEM)
    smem = pl.BlockSpec(memory_space=pltpu.SMEM)
    v = pltpu.VMEM
    dma = pltpu.SemaphoreType.DMA
    peers = NT - 1
    scratch = [
        v((T, 2 * N), BF16), v((T, DW), BF16), v((NT, 2, 128), F32), v((NT, 2, 128), F32),
        v((CHUNKS, C, CW), BF16), v((CHUNKS, 128, CW), BF16), v((CHUNKS, 128, CW), BF16),
        v((CHUNKS, 3, 32, CW), BF16), v((CHUNKS, 4, 32, 128), BF16), v((CHUNKS, 3, 32, 128), BF16),
        v((T, 2 * N), BF16), v((peers, 16, 2 * N), BF16),
        v((4, 128), F32), v((4, 128), F32), v((4, 128), F32), v((3, 4, 128), F32),
        v((4, 128), F32), v((3, 4, 128), F32),
        v((16, T), F32), v((16, T), F32), v((T, T), F32), v((T, T), BF16),
        v((C, T), F32), v((C, T), BF16), v((C, T), F32), v((C, T), F32), v((C, T), F32),
        v((C, T), F32), v((NH, T, T), BF16), v((NH, T, T), BF16), v((T, T), BF16),
        v((T, T), F32), v((C, T), F32), v((C, T), BF16), v((C, T), F32),
    ]
    counts = [peers, 17, peers, peers, CHUNKS, 3 * CHUNKS, 3 * CHUNKS, 3 * CHUNKS, 3 * CHUNKS,
              CHUNKS, peers, 7]
    for n in counts:
        scratch += [dma((n,)), dma((n,))]
    out = jax.ShapeDtypeStruct
    gx, gz, gdt, gb, gc, gw, gn, gs = pl.pallas_call(
        kernel,
        out_shape=(
            out((T, C), BF16), out((T, C), BF16), out((NH, T), F32), out((16, N), F32),
            out((16, N), F32), out((C, DW), BF16), out((2, 128), F32), out((1, 128), F32),
        ),
        in_specs=[vmem] * 5 + [smem] * 3 + [vmem] * 4,
        out_specs=(vmem,) * 8,
        scratch_shapes=scratch,
        compiler_params=pltpu.CompilerParams(
            collective_id=0, has_side_effects=True, vmem_limit_bytes=48 * 1024 * 1024
        ),
        cost_estimate=pl.CostEstimate(
            flops=2 * 10**9, bytes_accessed=4 * 2**20, transcendentals=10**6
        ),
    )(x, z, dt, b, c, a_log, skip, bias, gain.reshape(1, C), w, g, ids.reshape(1, T))
    return (
        gx, gz, gdt, gb, gc, gw, gn.reshape(C), gs[0, 4:8], gs[0, 0:4], gs[0, 8:12],
    )


def solution(mesh):
    in_specs = (
        P("dp", "tensor"),
        P("dp", "tensor"),
        P("tensor", "dp"),
        P(("dp", "tensor"), None),
        P(("dp", "tensor"), None),
        P("tensor"),
        P("tensor"),
        P("tensor"),
        P("tensor"),
        P("tensor", None),
        P(("dp", "tensor"), None),
        P("dp"),
    )
    out_specs = (
        P("dp", "tensor"),
        P("dp", "tensor"),
        P("tensor", "dp"),
        P(("dp", "tensor"), None),
        P(("dp", "tensor"), None),
        P("tensor", None),
        P("tensor"),
        P("tensor"),
        P("tensor"),
        P("tensor"),
    )
    return jax.shard_map(
        per_device, mesh=mesh, in_specs=in_specs, out_specs=out_specs, check_vma=False
    )
```

time: 679 us -> 83.3 us (0.12)
  blocking collectives: 356 us -> 0 us
  waiting for transfers between devices: 261 us -> 0 us
  Pallas kernels: 0 us -> 70.4 us
  other arithmetic: 19.8 us -> 0 us
  between operations: 14.3 us -> 0.71 us
  matrix products: 12.5 us -> 0 us
    psum x3 -> x0, blocking collectives: 263 us -> none  [the longest x1 178 us: per_device(): lax.psum((weight_acc, norm_grad, grad_al, grad_sk, grad_db), 'dp')]
    reduce_scatter x2 -> x0, waiting for transfers between devices: 261 us -> none  [the longest x1 218 us: per_device(): lax.psum_scatter(grad_bf, 'tensor', scatter_dimension=0, tiled=True)]
    all_gather x2 -> x0, blocking collectives: 92.9 us -> none  [the longest x1 51.3 us: per_device(): lax.all_gather(b_rows, 'tensor', axis=0, tiled=True)]
    pallas_call x0 -> x1, Pallas kernels: none -> 70.4 us  [per_device(): pl.pallas_call(kernel, out_shape=(out((T, C), BF16), out((T, C), BF16), o...]
    dot_general x14 -> x0, matrix products: 12.5 us -> none  [the longest x3 5.37 us: ssd_gate(): jnp.einsum('hcij,cjhp->cihp', mixing.astype(low), x_low, preferred_elemen...]
    unnamed x66 -> x31, local copies, waits for them, and re-layouts: 2.83 us -> 11.2 us
  transfers between devices with their start and end apart: 3 -> 0, of which waited for: 2 -> 0; matrix products, arithmetic and copies ran while one was open for 4% -> 0% of each run, Pallas kernels for 0% -> 0%
where the time goes in v1:
time: 83.3 us; the launch traced here: 83 us
  Pallas kernels  70.4 us (85%)
  local copies, waits for them, and re-layouts  11.8 us (14%)
    pallas_call x1, Pallas kernels, per_device(): pl.pallas_call(kernel, out_shape=(out((T, C), BF16), out((T, C), BF16), o...  70.4 us
    unnamed x31, local copies, waits for them, and re-layouts  11.2 us

profile of v1, /device:TPU:1, one launch (start us, length us, event | category | flops | bytes accessed | tf_op | source)
XLA Modules:
  0.0 83.0 jit_solution(1095866303070545992)
XLA Ops:
  0.6 0.0 copy-start.8
  0.7 0.0 copy-start.10
  0.7 0.0 copy-start.11
  0.7 0.0 copy-start.7
  0.7 0.6 copy-done.8
  1.3 0.0 copy-done.11
  1.3 0.0 copy-done.7
  1.4 0.0 copy-done.9
  1.4 1.2 %copy-done = bf16[256,2048]{1,0:T(8,128)(2,1)S(1)} copy-done((bf16[256,2048]{1,0:T(8,128)(2,1)S(1)}, bf16[256,2048]{1,0:T(8,128)(2,1)}, u32[]{:S(2)}) %copy-start) | copy-done | bytes 1048600
  2.6 0.9 %copy-done.1 = bf16[256,256]{1,0:T(8,128)(2,1)S(1)} copy-done((bf16[256,256]{1,0:T(8,128)(2,1)S(1)}, bf16[256,256]{1,0:T(8,128)(2,1)}, u32[]{:S(2)}) %copy-start.1) | copy-done | bytes 131096
  3.5 0.9 %copy-done.2 = bf16[256,256]{1,0:T(8,128)(2,1)S(1)} copy-done((bf16[256,256]{1,0:T(8,128)(2,1)S(1)}, bf16[256,256]{1,0:T(8,128)(2,1)}, u32[]{:S(2)}) %copy-start.2) | copy-done | bytes 131096
  4.4 0.8 %copy-done.3 = bf16[16,2048]{1,0:T(8,128)(2,1)S(1)} copy-done((bf16[16,2048]{1,0:T(8,128)(2,1)S(1)}, bf16[16,2048]{1,0:T(8,128)(2,1)}, u32[]{:S(2)}) %copy-start.3) | copy-done | bytes 65560
  5.3 0.7 copy-done.4
  5.9 0.7 copy-done.5
  6.6 0.7 copy-done.6
  7.3 70.4 %shard_map.195 = (bf16[256,256]{1,0:T(8,128)(2,1)S(1)}, bf16[256,256]{1,0:T(8,128)(2,1)S(1)}, f32[4,256]{1,0:T(4,128)S(1)}, f32[16,128]{1,0:T(8,128)S(1)}, f32[1...) custom-call(bf16[256,256]{1,0:T(8,128)(2,1)S(1)} %copy-done.1, ...), custom_call_target="tpu_custom_call" | custom-call | flops 2000000000 | bytes 4194304 | tf_op jit(solution)/shard_map/pallas_call | solution.py:418
  77.7 0.6 slice_bitcast_fusion
  78.3 0.7 copy.29
  79.0 0.7 copy.30
  79.6 0.6 copy.31
  80.2 0.6 copy.32
  80.8 0.6 copy.33
  81.4 1.0 %copy.34 = bf16[256,2048]{1,0:T(8,128)(2,1)} copy(bf16[256,2048]{1,0:T(8,128)(2,1)S(1)} %get-tuple-element.44) | data formatting | bytes 2097152
  82.4 0.6 copy.35
  (9 shorter events, 0.0 us)
Async XLA Ops:
  0.6 0.7 copy-start.8
  0.7 0.7 copy-start.10
  0.7 0.7 copy-start.11
  0.7 0.7 copy-start.7
  0.7 0.7 copy-start.9
  1.4 1.2 %copy-start = (bf16[256,2048]{1,0:T(8,128)(2,1)S(1)}, bf16[256,2048]{1,0:T(8,128)(2,1)}, u32[]{:S(2)}) copy-start(bf16[256,2048]{1,0:T(8,128)(2,1)} %w_ref.1) | copy-start | bytes 3145732
  2.6 0.9 %copy-start.1 = (bf16[256,256]{1,0:T(8,128)(2,1)S(1)}, bf16[256,256]{1,0:T(8,128)(2,1)}, u32[]{:S(2)}) copy-start(bf16[256,256]{1,0:T(8,128)(2,1)} %x_ref.1) | copy-start | bytes 393220
  3.5 0.9 %copy-start.2 = (bf16[256,256]{1,0:T(8,128)(2,1)S(1)}, bf16[256,256]{1,0:T(8,128)(2,1)}, u32[]{:S(2)}) copy-start(bf16[256,256]{1,0:T(8,128)(2,1)} %z_ref.1) | copy-start | bytes 393220
  4.4 0.8 %copy-start.3 = (bf16[16,2048]{1,0:T(8,128)(2,1)S(1)}, bf16[16,2048]{1,0:T(8,128)(2,1)}, u32[]{:S(2)}) copy-start(bf16[16,2048]{1,0:T(8,128)(2,1)} %g_ref.1) | copy-start | bytes 196612
  5.3 0.7 copy-start.4
  5.9 0.7 copy-start.5
  6.6 0.7 copy-start.6

commit v2 on v1

v2 whole, which is shorter than its diff:
```python
import jax
import jax.numpy as jnp
from jax import lax
from jax.experimental import pallas as pl
from jax.experimental.pallas import tpu as pltpu
from jax.sharding import PartitionSpec as P

MESH = pl.DeviceIdType.MESH
HI = lax.Precision.HIGHEST
F32 = jnp.float32
BF16 = jnp.bfloat16
EPS = 1e-05

T = 256
C = 256
HD = 64
NH = 4
N = 128
DW = 2048
NT = 16
NY = 8
CHUNKS = 4
CW = DW // CHUNKS
ROUTE = ("xz", "xz", "zx", "xz")
ORDER = (0, 1, 2, 3)
INNER = C * NT


def nn(a, b, prec=None):
    return lax.dot_general(a, b, (((1,), (0,)), ((), ())), precision=prec, preferred_element_type=F32)


def nt(a, b, prec=None):
    return lax.dot_general(a, b, (((1,), (1,)), ((), ())), precision=prec, preferred_element_type=F32)


def tn(a, b, prec=None):
    return lax.dot_general(a, b, (((0,), (0,)), ((), ())), precision=prec, preferred_element_type=F32)


def kernel(
    x_hbm, z_hbm, dt_hbm, b_hbm, c_hbm, al_hbm, sk_hbm, db_hbm, gain_hbm, w_hbm, g_hbm, ids_hbm,
    gx_ref, gz_ref, gdt_ref, gb_ref, gc_ref, gw_ref, gn_ref, gal_ref, gsk_ref, gdb_ref,
    bc, gall, st1, st2, wk, r1, s2, r2, s3, r3, dbc, dbr, pk, p1, p2, p3,
    x_ref, z_ref, dt_ref, al_ref, sk_ref, db_ref, gain_ref, w_ref, ids_ref,
    rw, pr, mb, tge, xt, xtb, silt, dst, yt, gt, ks, hs, qs, ws, dxt, nrm, mx,
    in_s, bc_s, bc_r, g_s, g_r, st1_s, st1_r, st2_s, st2_r, c_s, c_r, x_s, x_r, z_s, z_r,
    az_s, az_r, ax_s, ax_r, ac_s, ac_r, db_s, db_r, p_s, p_r,
):
    dp = lax.axis_index("dp")
    me = lax.axis_index("tensor")
    zl, xi, core = dp // 8, (dp // 2) % 4, dp % 2
    y, zh = me // 2, me % 2

    def at_x(o):
        return zl * 8 + ((xi + o) % 4) * 2 + core

    def at_z(o):
        return ((zl + o) % 4) * 8 + xi * 2 + core

    other_core = zl * 8 + xi * 2 + (1 - core)
    dp_peers = [other_core] + [at_x(o) for o in (1, 2, 3)] + [at_z(o) for o in (1, 2, 3)]

    barrier = pltpu.get_barrier_semaphore()
    for o in range(1, NT):
        pl.semaphore_signal(barrier, inc=1, device_id=(dp, (me + o) % NT), device_id_type=MESH)
    for peer in dp_peers:
        pl.semaphore_signal(barrier, inc=1, device_id=(peer, me), device_id_type=MESH)

    def send(src, dst, ss, rs, dev):
        copy = pltpu.make_async_remote_copy(
            src_ref=src, dst_ref=dst, send_sem=ss, recv_sem=rs, device_id=dev, device_id_type=MESH
        )
        copy.start()
        return copy

    def both(ref, ss, rs):
        return pltpu.make_async_remote_copy(
            src_ref=ref, dst_ref=ref, send_sem=ss, recv_sem=rs,
            device_id=(other_core, me), device_id_type=MESH,
        )

    sent = []

    def rows(i, n):
        return pl.ds(pl.multiple_of(i * n, n), n)

    loads = [
        pltpu.make_async_copy(src, dst, in_s.at[i])
        for i, (src, dst) in enumerate([
            (b_hbm, bc.at[rows(me, 16), 0:N]), (c_hbm, bc.at[rows(me, 16), N:2 * N]),
            (g_hbm, gall.at[rows(me, 16), :]), (al_hbm, al_ref), (sk_hbm, sk_ref),
            (db_hbm, db_ref), (dt_hbm, dt_ref), (gain_hbm, gain_ref), (ids_hbm, ids_ref),
            (x_hbm, x_ref), (z_hbm, z_ref), (w_hbm, w_ref),
        ])
    ]
    for load in loads:
        load.start()
    for load in loads[:3]:
        load.wait()

    pl.semaphore_wait(barrier, NT - 1 + len(dp_peers))

    g_copies = {}
    spans = {0: (1, 2, 3, 4, -1, -2, -3), 1: (1, 2, 3, -1, -2, -3, -4)}

    def piece(slot):
        return gall.at[rows(slot, 16), :]

    def push(kind, slot, hop, span):
        i = 1 + kind * 7 + spans[kind].index(span)
        to = ((y + hop + NY) % NY) * 2 + zh
        g_copies[kind, span] = send(piece(slot), piece(slot), g_s.at[0], g_r.at[i], (dp, to))

    def direct(kind, slot):
        for d in (2, -2, 1, -1):
            push(kind, slot, d, d)

    def forward(kind):
        half = zh if kind == 0 else 1 - zh
        for d in (1, -1):
            g_copies[kind, 2 * d].wait_recv()
            slot = ((y - 2 * d + NY) % NY) * 2 + half
            if 4 * d in spans[kind]:
                push(kind, slot, 2 * d, 4 * d)
            push(kind, slot, d, 3 * d)

    partner = y * 2 + 1 - zh
    zcopy = send(piece(me), piece(me), g_s.at[0], g_r.at[0], (dp, partner))
    far = sorted(range(1, NT), key=lambda o: -min(o // 2, NY - o // 2))
    for o in far:
        mine = bc.at[rows(me, 16), :]
        send(mine, mine, bc_s.at[0], bc_r.at[0], (dp, (me + o) % NT))
    bc_all = both(bc.at[0:(NT - 1) * 16, :], bc_s.at[0], bc_r.at[0])
    sent.append(bc_all)

    direct(0, me)
    sent.append(both(gall.at[0:(NT - 1) * 16, :], g_s.at[0], g_r.at[0]))

    for load in loads[3:9]:
        load.wait()
    hrow = lax.broadcasted_iota(jnp.int32, (NH, T), 0)

    def per_head(ref):
        v = jnp.full((NH, T), ref[0], F32)
        for h in range(1, NH):
            v = jnp.where(hrow == h, ref[h], v)
        return v

    pre = dt_ref[...] + per_head(db_ref)
    step = jnp.maximum(pre, 0.0) + jnp.log1p(jnp.exp(-jnp.abs(pre)))
    sig = 1.0 / (1.0 + jnp.exp(-pre))
    ea = jnp.exp(per_head(al_ref))
    ld = -ea * step
    rw[...] = jnp.zeros_like(rw)
    rw[0:NH, :] = step
    rw[4:5, :] = ids_ref[...].astype(F32)
    rw[5:6, :] = gain_ref[...]
    rw[8:8 + NH, :] = ld
    ri = lax.broadcasted_iota(jnp.int32, (T, T), 0)
    ci = lax.broadcasted_iota(jnp.int32, (T, T), 1)
    tril = jnp.where(ri >= ci, 1.0, 0.0)
    eye = jnp.where(ri == ci, 1.0, 0.0)
    tge[...] = tril.astype(BF16)
    cols = nt(eye, rw[0:8, :], HI)
    cumc = nt(tril, rw[8:16, :], HI)
    cumr = nt(rw[8:16, :], tril, HI)
    idr = rw[4:5, :]
    mb[...] = jnp.where((ri <= ci) & (cols[:, 4:5] == idr), 0.0, -1e30)
    gain_col = cols[:, 5:6]

    for load in loads[9:]:
        load.wait()
    xv = x_ref[...].astype(F32).T
    xt[...] = xv
    xtb[...] = xv.astype(BF16)
    zv = z_ref[...].astype(F32).T
    sg = 1.0 / (1.0 + jnp.exp(-zv))
    silt[...] = zv * sg
    dst[...] = sg * (1.0 + zv * (1.0 - sg))

    ks[...] = jnp.zeros_like(ks)
    hs[...] = jnp.zeros_like(hs)

    zcopy.wait_recv()
    direct(1, partner)
    forward(0)
    bc_all.wait_recv()
    ball = bc[:, 0:N]
    call = bc[:, N:2 * N]
    scores = nt(ball, call)
    mx[...] = scores
    for h in range(NH):
        for s0 in range(0, T, 64):
            t0 = 0 if s0 < 128 else 128
            gap = cumr[h:h + 1, t0:] - cumc[s0:s0 + 64, h:h + 1] + mb[s0:s0 + 64, t0:]
            w = jnp.exp(gap) * cols[s0:s0 + 64, h:h + 1]
            hs[h, s0:s0 + 64, t0:] = w.astype(BF16)
            ks[h, s0:s0 + 64, t0:] = (w * mx[s0:s0 + 64, t0:]).astype(BF16)
        c0 = h * HD
        yv = nn(xtb[c0:c0 + HD, :], ks[h]) + sk_ref[h] * xt[c0:c0 + HD, :]
        yt[c0:c0 + HD, :] = yv
        gt[c0:c0 + HD, :] = yv * silt[c0:c0 + HD, :]

    def all_stats(st, row, ss, rs):
        st[me, 0:1, :] = row[:, 0:128]
        st[me, 1:2, :] = row[:, 128:256]
        for o in far:
            send(st.at[me], st.at[me], ss.at[0], rs.at[0], (dp, (me + o) % NT))
        sent.append(both(st.at[0:NT - 1], ss.at[0], rs.at[0]))
        return sent[-1]

    def sum_stats(st, copies):
        copies.wait_recv()
        tot = jnp.sum(st[...], axis=0)
        return jnp.concatenate([tot[0:1, :], tot[1:2, :]], axis=1)

    gated = gt[...]
    stat1 = all_stats(st1, jnp.sum(gated * gated, axis=0, keepdims=True), st1_s, st1_r)

    forward(1)
    for (_, span), copy in g_copies.items():
        if abs(span) != 2:
            copy.wait_recv()
    mixed = nt(w_ref[...], gall[...])
    mx[...] = mixed
    stat2 = all_stats(
        st2, jnp.sum(gt[...] * gain_col * mixed, axis=0, keepdims=True), st2_s, st2_r
    )

    inv = lax.rsqrt(sum_stats(st1, stat1) / INNER + EPS)
    nrm[...] = (gt[...] * inv * gain_col).astype(BF16)

    core_copies = {}
    for k in ORDER:
        wk[k] = nn(nrm[...], gall[:, k * CW:(k + 1) * CW]).astype(BF16)
        core_copies[k] = send(
            wk.at[k, rows(1 - core, 128), :], r1.at[k], c_s.at[0], c_r.at[k], (other_core, me)
        )
    sent.append(both(r1, c_s.at[0], c_r.at[0]))

    axes = {"x": (xi, at_x), "z": (zl, at_z)}
    def stage_x(k):
        core_copies[k].wait_recv()
        s2[k] = (wk[k, rows(core, 128), :].astype(F32) + r1[k].astype(F32)).astype(BF16)
        at, to = axes[ROUTE[k][0]]
        for o in (2, 1, 3):
            send(
                s2.at[k, rows((at + o) % 4, 32), :], r2.at[k, o - 1],
                x_s.at[0], x_r.at[k], (to(o), me),
            )

    def stage_z(k):
        both(r2.at[k], x_s.at[0], x_r.at[k]).wait_recv()
        at, _ = axes[ROUTE[k][0]]
        tot = s2[k, rows(at, 32), :].astype(F32)
        for o in range(3):
            tot = tot + r2[k, o].astype(F32)
        tot = tot.astype(BF16)
        for q in range(4):
            s3[k, q] = tot[:, q * 128:(q + 1) * 128]
        at, to = axes[ROUTE[k][1]]
        for o in (2, 1, 3):
            send(
                s3.at[k, (at + o) % 4], r3.at[k, o - 1], z_s.at[0], z_r.at[k], (to(o), me)
            )

    def gather_z(k):
        both(r3.at[k], z_s.at[0], z_r.at[k]).wait_recv()
        at, to = axes[ROUTE[k][1]]
        tot = s3[k, at].astype(F32)
        for o in range(3):
            tot = tot + r3[k, o].astype(F32)
        r0 = rows(core * 4 + axes[ROUTE[k][0]][0], 32)
        col = pl.ds(pl.multiple_of(k * CW + at * 128, 128), 128)
        gw_ref[r0, col] = tot.astype(BF16)
        for o in (2, 1, 3):
            send(
                gw_ref.at[r0, col], gw_ref.at[r0, col], az_s.at[0], az_r.at[k], (to(o), me)
            )

    def gather_x(k):
        both(r3.at[k], az_s.at[0], az_r.at[k]).wait_recv()
        at, to = axes[ROUTE[k][0]]
        block = gw_ref.at[rows(core * 4 + at, 32), k * CW:(k + 1) * CW]
        for o in (2, 1, 3):
            send(block, block, ax_s.at[0], ax_r.at[k], (to(o), me))

    def gather_core(k):
        both(r2.at[k], ax_s.at[0], ax_r.at[k]).wait_recv()
        block = gw_ref.at[rows(core, 128), k * CW:(k + 1) * CW]
        send(block, block, ac_s.at[0], ac_r.at[k], (other_core, me))

    def gather_end(k):
        both(r1.at[k], ac_s.at[0], ac_r.at[k]).wait_recv()

    sent.extend([
        both(r2, x_s.at[0], x_r.at[0]), both(r3, z_s.at[0], z_r.at[0]),
        both(r3, az_s.at[0], az_r.at[0]), both(r2, ax_s.at[0], ax_r.at[0]),
        both(r1, ac_s.at[0], ac_r.at[0]),
    ])

    for k in ORDER:
        stage_x(k)

    for k in ORDER:
        stage_z(k)
    slope = sum_stats(st2, stat2) / INNER
    mixed = mx[...]
    gated = gt[...]
    ng = nt(jnp.ones((8, T), F32), mixed * gated * inv, HI)
    ggt = gain_col * mixed * inv - gated * (inv * inv * inv * slope)
    gz_ref[...] = (ggt * yt[...] * dst[...]).T.astype(BF16)
    yt[...] = ggt * silt[...]

    ws[...] = jnp.zeros_like(ws)
    qs[...] = jnp.zeros_like(qs)
    pr[...] = jnp.zeros_like(pr)
    strict = jnp.where(ri < ci, 1.0, 0.0)

    def back(h):
        c0 = h * HD
        dy = yt[c0:c0 + HD, :]
        xh = xt[c0:c0 + HD, :]
        dyb = dy.astype(BF16)
        for s0, t0 in ((0, 0), (128, 128)):
            dm = tn(xtb[c0:c0 + HD, s0:s0 + 128], dyb[:, t0:])
            qs[s0:s0 + 128, t0:] = (dm * ks[h, s0:s0 + 128, t0:].astype(F32)).astype(BF16)
            ws[s0:s0 + 128, t0:] += dm * hs[h, s0:s0 + 128, t0:].astype(F32)
        top = jnp.sum(nn(qs[0:128, :], tge[...]) * strict[0:128, :], axis=0, keepdims=True)
        low = jnp.sum(
            nn(qs[128:, 128:], tge[128:, 128:]) * strict[128:, 128:], axis=0, keepdims=True
        )
        dld = jnp.concatenate([top[:, 0:128], top[:, 128:] + low], axis=1)
        dxi = nt(dyb, ks[h])
        direct = jnp.sum(xh * dxi, axis=0, keepdims=True) / rw[h:h + 1, :]
        dxt[c0:c0 + HD, :] = dxi + sk_ref[h] * dy
        pr[h:h + 1, :] = jnp.sum(dy * xh, axis=0, keepdims=True)
        pr[4 + h:5 + h, :] = dld
        pr[8 + h:9 + h, :] = direct

    for h in range(NH):
        back(h)

    dld = pr[4:8, :]
    ddt = (pr[8:12, :] - ea * dld) * sig
    gdt_ref[...] = ddt
    pr[4:8, :] = dld * ld
    pr[8:12, :] = ddt

    wb = ws[...].astype(BF16)
    dbc[:, 0:N] = nn(wb, call).astype(BF16)
    dbc[:, N:2 * N] = tn(wb, ball).astype(BF16)
    for o in far:
        send(
            dbc.at[rows((me + o) % NT, 16), :], dbr.at[o - 1],
            db_s.at[0], db_r.at[0], (dp, (me + o) % NT),
        )
    d_all = both(dbr, db_s.at[0], db_r.at[0])
    sent.append(d_all)

    ones = jnp.ones((8, T), F32)
    pk[...] = jnp.zeros_like(pk)
    pk[0:1, :] = ng[0:1, 0:128]
    pk[1:2, :] = ng[0:1, 128:256]
    for q in range(3):
        pk[2 + q:3 + q, 0:NH] = nt(ones, pr[4 * q:4 * q + 4, :], HI)[0:1, :]
    pc = send(pk, p1, p_s.at[0], p_r.at[0], (other_core, me))

    for k in ORDER:
        gather_z(k)
    pc.wait_recv()
    p2[xi] = pk[...] + p1[...]
    for o in (1, 2, 3):
        send(p2.at[xi], p2.at[xi], p_s.at[1], p_r.at[1], (at_x(o), me))
    px = both(p2.at[0:3], p_s.at[1], p_r.at[1])
    gx_ref[...] = dxt[...].T.astype(BF16)
    for k in ORDER:
        gather_x(k)
    px.wait_recv()
    p3[zl] = p2[0] + p2[1] + p2[2] + p2[3]
    for o in (1, 2, 3):
        send(p3.at[zl], p3.at[zl], p_s.at[2], p_r.at[2], (at_z(o), me))
    pz = both(p3.at[0:3], p_s.at[2], p_r.at[2])
    sent.extend([pc, px, pz])
    d_all.wait_recv()
    tot = dbc[rows(me, 16), :].astype(F32)
    for o in range(NT - 1):
        tot = tot + dbr[o].astype(F32)
    gb_ref[...] = tot[:, 0:N]
    gc_ref[...] = tot[:, N:2 * N]
    for k in ORDER:
        gather_core(k)
    pz.wait_recv()
    tot = p3[0] + p3[1] + p3[2] + p3[3]
    gn_ref[...] = tot[0:2, :]
    gsk_ref[...] = tot[2, 0:NH]
    gal_ref[...] = tot[3, 0:NH]
    gdb_ref[...] = tot[4, 0:NH]
    for k in ORDER:
        gather_end(k)
    for copy in sent:
        copy.wait_send()


def finish(*refs):
    n = (len(refs) - 1) // 2
    copies = [pltpu.make_async_copy(refs[i], refs[n + i], refs[-1].at[i]) for i in range(n)]
    for copy in copies:
        copy.start()
    for copy in copies:
        copy.wait()


def per_device(x, z, dt, b, c, a_log, skip, bias, gain, w, g, ids):
    v = pltpu.VMEM
    dma = pltpu.SemaphoreType.DMA
    peers = NT - 1
    scratch = [
        v((T, 2 * N), BF16), v((T, DW), BF16), v((NT, 2, 128), F32), v((NT, 2, 128), F32),
        v((CHUNKS, C, CW), BF16), v((CHUNKS, 128, CW), BF16), v((CHUNKS, 128, CW), BF16),
        v((CHUNKS, 3, 32, CW), BF16), v((CHUNKS, 4, 32, 128), BF16), v((CHUNKS, 3, 32, 128), BF16),
        v((T, 2 * N), BF16), v((peers, 16, 2 * N), BF16),
        v((8, 128), F32), v((8, 128), F32), v((4, 8, 128), F32), v((4, 8, 128), F32),
        v((T, C), BF16), v((T, C), BF16), v((NH, T), F32), pltpu.SMEM((NH,), F32),
        pltpu.SMEM((NH,), F32), pltpu.SMEM((NH,), F32), v((1, C), F32), v((C, DW), BF16),
        v((1, T), jnp.int32),
        v((16, T), F32), v((16, T), F32), v((T, T), F32), v((T, T), BF16),
        v((C, T), F32), v((C, T), BF16), v((C, T), F32), v((C, T), F32), v((C, T), F32),
        v((C, T), F32), v((NH, T, T), BF16), v((NH, T, T), BF16), v((T, T), BF16),
        v((T, T), F32), v((C, T), F32), v((C, T), BF16), v((C, T), F32),
        dma((12,)),
    ]
    counts = [(1, 1), (1, 17), (1, 1), (1, 1)] + [(1, CHUNKS)] * 6 + [(1, 1), (3, 3)]
    for n in counts:
        scratch += [dma((n[0],)), dma((n[1],))]
    out = jax.ShapeDtypeStruct
    vmem = pl.BlockSpec(memory_space=pltpu.VMEM)
    anywhere = pl.BlockSpec(memory_space=pl.ANY)
    small = out((NH,), F32)
    results = pl.pallas_call(
        kernel,
        out_shape=(
            out((T, C), BF16), out((T, C), BF16), out((NH, T), F32), out((16, N), F32),
            out((16, N), F32), out((C, DW), BF16), out((2, 128), F32), small, small, small,
        ),
        in_specs=[anywhere] * 12,
        out_specs=(vmem,) * 10,
        scratch_shapes=scratch,
        compiler_params=pltpu.CompilerParams(
            collective_id=0, has_side_effects=True, vmem_limit_bytes=56 * 1024 * 1024
        ),
        cost_estimate=pl.CostEstimate(
            flops=2 * 10**9, bytes_accessed=4 * 2**20, transcendentals=10**6
        ),
    )(x, z, dt, b, c, a_log, skip, bias, gain.reshape(1, C), w, g, ids.reshape(1, T))
    results = pl.pallas_call(
        finish,
        out_shape=tuple(out(r.shape, r.dtype) for r in results),
        in_specs=[vmem] * 10,
        out_specs=(anywhere,) * 10,
        scratch_shapes=[dma((10,))],
    )(*results)
    gx, gz, gdt, gb, gc, gw, gn, gal, gsk, gdb = results
    return gx, gz, gdt, gb, gc, gw, gn.reshape(C), gal, gsk, gdb


def solution(mesh):
    in_specs = (
        P("dp", "tensor"),
        P("dp", "tensor"),
        P("tensor", "dp"),
        P(("dp", "tensor"), None),
        P(("dp", "tensor"), None),
        P("tensor"),
        P("tensor"),
        P("tensor"),
        P("tensor"),
        P("tensor", None),
        P(("dp", "tensor"), None),
        P("dp"),
    )
    out_specs = (
        P("dp", "tensor"),
        P("dp", "tensor"),
        P("tensor", "dp"),
        P(("dp", "tensor"), None),
        P(("dp", "tensor"), None),
        P("tensor", None),
        P("tensor"),
        P("tensor"),
        P("tensor"),
        P("tensor"),
    )
    return jax.shard_map(
        per_device, mesh=mesh, in_specs=in_specs, out_specs=out_specs, check_vma=False
    )
```

time: 83.3 us -> 66.1 us (0.79)
  local copies, waits for them, and re-layouts: 11.8 us -> 0 us
  Pallas kernels: 70.4 us -> 65.3 us
    unnamed x31 -> x0, local copies, waits for them, and re-layouts: 11.2 us -> none
    pallas_call x1, Pallas kernels: 70.4 us -> 62.8 us  [per_device(): pl.pallas_call(kernel, out_shape=(out((T, C), BF16), out((T, C), BF16), o...]
    pallas_call x0 -> x1, Pallas kernels: none -> 2.46 us  [per_device(): pl.pallas_call(finish, out_shape=tuple((out(r.shape, r.dtype) for r in re...]
where the time goes in v2:
time: 66.1 us; the launch traced here: 65.9 us
  Pallas kernels  65.3 us (99%)
    pallas_call x1, Pallas kernels, per_device(): pl.pallas_call(kernel, out_shape=(out((T, C), BF16), out((T, C), BF16), o...  62.8 us
    pallas_call x1, Pallas kernels, per_device(): pl.pallas_call(finish, out_shape=tuple((out(r.shape, r.dtype) for r in re...  2.46 us

profile of v2, /device:TPU:1, one launch (start us, length us, event | category | flops | bytes accessed | tf_op | source)
XLA Modules:
  0.0 65.9 jit_solution(8602705740044606534)
XLA Ops:
  0.6 62.8 %shard_map.195 = (bf16[256,256]{1,0:T(8,128)(2,1)}, bf16[256,256]{1,0:T(8,128)(2,1)}, f32[4,256]{1,0:T(4,128)}, f32[16,128]{1,0:T(8,128)}, f32[16,128]{1,0:T(8,1...) custom-call(bf16[256,256]{1,0:T(8,128)(2,1)} %x_hbm.1, ...), custom_call_target="tpu_custom_call" | custom-call | flops 2000000000 | bytes 4194304 | tf_op jit(solution)/shard_map/pallas_call | solution.py:441
  63.5 2.5 %shard_map.196 = (bf16[256,256]{1,0:T(8,128)(2,1)}, bf16[256,256]{1,0:T(8,128)(2,1)}, f32[4,256]{1,0:T(4,128)}, f32[16,128]{1,0:T(8,128)}, f32[16,128]{1,0:T(8,1...) custom-call(bf16[256,256]{1,0:T(8,128)(2,1)} %get-tuple-element.30.refs_0_, ...), custom_call_target="tpu_custom_call" | custom-call | tf_op jit(solution)/shard_map/pallas_call | solution.py:457

commit v3 on v2

--- a/solution.py
+++ b/solution.py
@@ -21,8 +21,9 @@
 NY = 8
 CHUNKS = 4
 CW = DW // CHUNKS
+HW = DW // 2
 ROUTE = ("xz", "xz", "zx", "xz")
-ORDER = (0, 1, 2, 3)
+WHOLE = (False, False, True, True)
 INNER = C * NT
 
 
@@ -41,7 +42,7 @@
 def kernel(
     x_hbm, z_hbm, dt_hbm, b_hbm, c_hbm, al_hbm, sk_hbm, db_hbm, gain_hbm, w_hbm, g_hbm, ids_hbm,
     gx_ref, gz_ref, gdt_ref, gb_ref, gc_ref, gw_ref, gn_ref, gal_ref, gsk_ref, gdb_ref,
-    bc, gall, st1, st2, wk, r1, s2, r2, s3, r3, dbc, dbr, pk, p1, p2, p3,
+    bc, gall, st1, st2, wk, r1, s2, r2, s3, s4, r3, dbc, dbr, pk, p1, p2, p3,
     x_ref, z_ref, dt_ref, al_ref, sk_ref, db_ref, gain_ref, w_ref, ids_ref,
     rw, pr, mb, tge, xt, xtb, silt, dst, yt, gt, ks, hs, qs, ws, dxt, nrm, mx,
     in_s, bc_s, bc_r, g_s, g_r, st1_s, st1_r, st2_s, st2_r, c_s, c_r, x_s, x_r, z_s, z_r,
@@ -102,31 +103,44 @@
     pl.semaphore_wait(barrier, NT - 1 + len(dp_peers))
 
     g_copies = {}
+    z_copies = {}
     spans = {0: (1, 2, 3, 4, -1, -2, -3), 1: (1, 2, 3, -1, -2, -3, -4)}
-
-    def piece(slot):
-        return gall.at[rows(slot, 16), :]
-
-    def push(kind, slot, hop, span):
-        i = 1 + kind * 7 + spans[kind].index(span)
+    partner = y * 2 + 1 - zh
+
+    def piece(slot, part):
+        return gall.at[rows(slot, 16), part * HW:(part + 1) * HW]
+
+    def push(part, kind, slot, hop, span):
+        i = part * 15 + 1 + kind * 7 + spans[kind].index(span)
         to = ((y + hop + NY) % NY) * 2 + zh
-        g_copies[kind, span] = send(piece(slot), piece(slot), g_s.at[0], g_r.at[i], (dp, to))
-
-    def direct(kind, slot):
+        mine = piece(slot, part)
+        g_copies[part, kind, span] = send(mine, mine, g_s.at[part], g_r.at[i], (dp, to))
+
+    def cross(part):
+        mine = piece(me, part)
+        z_copies[part] = send(mine, mine, g_s.at[part], g_r.at[part * 15], (dp, partner))
+
+    def direct(part, kind):
+        if kind:
+            z_copies[part].wait_recv()
         for d in (2, -2, 1, -1):
-            push(kind, slot, d, d)
-
-    def forward(kind):
+            push(part, kind, partner if kind else me, d, d)
+
+    def forward(part, kind):
         half = zh if kind == 0 else 1 - zh
         for d in (1, -1):
-            g_copies[kind, 2 * d].wait_recv()
+            g_copies[part, kind, 2 * d].wait_recv()
             slot = ((y - 2 * d + NY) % NY) * 2 + half
             if 4 * d in spans[kind]:
-                push(kind, slot, 2 * d, 4 * d)
-            push(kind, slot, d, 3 * d)
-
-    partner = y * 2 + 1 - zh
-    zcopy = send(piece(me), piece(me), g_s.at[0], g_r.at[0], (dp, partner))
+                push(part, kind, slot, 2 * d, 4 * d)
+            push(part, kind, slot, d, 3 * d)
+
+    def arrived(part):
+        for (p, _, span), copy in g_copies.items():
+            if p == part and abs(span) != 2:
+                copy.wait_recv()
+
+    cross(0)
     far = sorted(range(1, NT), key=lambda o: -min(o // 2, NY - o // 2))
     for o in far:
         mine = bc.at[rows(me, 16), :]
@@ -134,8 +148,10 @@
     bc_all = both(bc.at[0:(NT - 1) * 16, :], bc_s.at[0], bc_r.at[0])
     sent.append(bc_all)
 
-    direct(0, me)
-    sent.append(both(gall.at[0:(NT - 1) * 16, :], g_s.at[0], g_r.at[0]))
+    direct(0, 0)
+    cross(1)
+    for part in (0, 1):
+        sent.append(both(gall.at[0:(NT - 1) * 16, 0:HW], g_s.at[part], g_r.at[part * 15]))
 
     for load in loads[3:9]:
         load.wait()
@@ -180,11 +196,15 @@
     dst[...] = sg * (1.0 + zv * (1.0 - sg))
 
     ks[...] = jnp.zeros_like(ks)
-    hs[...] = jnp.zeros_like(hs)
-
-    zcopy.wait_recv()
-    direct(1, partner)
-    forward(0)
+    for h in range(NH):
+        for s0 in range(0, T, 64):
+            t0 = 0 if s0 < 128 else 128
+            gap = cumr[h:h + 1, t0:] - cumc[s0:s0 + 64, h:h + 1] + mb[s0:s0 + 64, t0:]
+            hs[h, s0:s0 + 64, t0:] = jnp.exp(gap) * cols[s0:s0 + 64, h:h + 1]
+
+    direct(0, 1)
+    forward(0, 0)
+    direct(1, 0)
     bc_all.wait_recv()
     ball = bc[:, 0:N]
     call = bc[:, N:2 * N]
@@ -193,10 +213,9 @@
     for h in range(NH):
         for s0 in range(0, T, 64):
             t0 = 0 if s0 < 128 else 128
-            gap = cumr[h:h + 1, t0:] - cumc[s0:s0 + 64, h:h + 1] + mb[s0:s0 + 64, t0:]
-            w = jnp.exp(gap) * cols[s0:s0 + 64, h:h + 1]
-            hs[h, s0:s0 + 64, t0:] = w.astype(BF16)
-            ks[h, s0:s0 + 64, t0:] = (w * mx[s0:s0 + 64, t0:]).astype(BF16)
+            ks[h, s0:s0 + 64, t0:] = (
+                hs[h, s0:s0 + 64, t0:] * mx[s0:s0 + 64, t0:]
+            ).astype(BF16)
         c0 = h * HD
         yv = nn(xtb[c0:c0 + HD, :], ks[h]) + sk_ref[h] * xt[c0:c0 + HD, :]
         yt[c0:c0 + HD, :] = yv
@@ -218,25 +237,23 @@
     gated = gt[...]
     stat1 = all_stats(st1, jnp.sum(gated * gated, axis=0, keepdims=True), st1_s, st1_r)
 
-    forward(1)
-    for (_, span), copy in g_copies.items():
-        if abs(span) != 2:
-            copy.wait_recv()
-    mixed = nt(w_ref[...], gall[...])
-    mx[...] = mixed
-    stat2 = all_stats(
-        st2, jnp.sum(gt[...] * gain_col * mixed, axis=0, keepdims=True), st2_s, st2_r
-    )
-
+    forward(0, 1)
+    direct(1, 1)
+    forward(1, 0)
+    arrived(0)
+    mx[...] = nt(w_ref[:, 0:HW], gall[:, 0:HW])
+    forward(1, 1)
     inv = lax.rsqrt(sum_stats(st1, stat1) / INNER + EPS)
     nrm[...] = (gt[...] * inv * gain_col).astype(BF16)
 
     core_copies = {}
-    for k in ORDER:
+
+    def weight(k):
         wk[k] = nn(nrm[...], gall[:, k * CW:(k + 1) * CW]).astype(BF16)
         core_copies[k] = send(
             wk.at[k, rows(1 - core, 128), :], r1.at[k], c_s.at[0], c_r.at[k], (other_core, me)
         )
+
     sent.append(both(r1, c_s.at[0], c_r.at[0]))
 
     axes = {"x": (xi, at_x), "z": (zl, at_z)}
@@ -257,16 +274,30 @@
         for o in range(3):
             tot = tot + r2[k, o].astype(F32)
         tot = tot.astype(BF16)
+        at, to = axes[ROUTE[k][1]]
+        if WHOLE[k]:
+            mine = s4.at[k, at]
+            s4[k, at] = tot
+            for o in (2, 1, 3):
+                send(mine, mine, z_s.at[k], z_r.at[k], (to(o), me))
+            return
         for q in range(4):
             s3[k, q] = tot[:, q * 128:(q + 1) * 128]
-        at, to = axes[ROUTE[k][1]]
         for o in (2, 1, 3):
             send(
-                s3.at[k, (at + o) % 4], r3.at[k, o - 1], z_s.at[0], z_r.at[k], (to(o), me)
+                s3.at[k, (at + o) % 4], r3.at[k, o - 1], z_s.at[k], z_r.at[k], (to(o), me)
             )
 
     def gather_z(k):
-        both(r3.at[k], z_s.at[0], z_r.at[k]).wait_recv()
+        both(s4.at[k, 0:3] if WHOLE[k] else r3.at[k], z_s.at[k], z_r.at[k]).wait_recv()
+        if WHOLE[k]:
+            tot = s4[k, 0].astype(F32)
+            for q in range(1, 4):
+                tot = tot + s4[k, q].astype(F32)
+            r0 = rows(core * 4 + axes[ROUTE[k][0]][0], 32)
+            gw_ref[r0, k * CW:(k + 1) * CW] = tot.astype(BF16)
+            gather_x(k)
+            return
         at, to = axes[ROUTE[k][1]]
         tot = s3[k, at].astype(F32)
         for o in range(3):
@@ -280,7 +311,8 @@
             )
 
     def gather_x(k):
-        both(r3.at[k], az_s.at[0], az_r.at[k]).wait_recv()
+        if not WHOLE[k]:
+            both(r3.at[k], az_s.at[0], az_r.at[k]).wait_recv()
         at, to = axes[ROUTE[k][0]]
         block = gw_ref.at[rows(core * 4 + at, 32), k * CW:(k + 1) * CW]
         for o in (2, 1, 3):
@@ -295,16 +327,30 @@
         both(r1.at[k], ac_s.at[0], ac_r.at[k]).wait_recv()
 
     sent.extend([
-        both(r2, x_s.at[0], x_r.at[0]), both(r3, z_s.at[0], z_r.at[0]),
-        both(r3, az_s.at[0], az_r.at[0]), both(r2, ax_s.at[0], ax_r.at[0]),
+        both(s4.at[k, 0:3] if WHOLE[k] else r3.at[k], z_s.at[k], z_r.at[k]) for k in range(CHUNKS)
+    ])
+    sent.extend([
+        both(r2, x_s.at[0], x_r.at[0]), both(r3.at[0:WHOLE.count(False)], az_s.at[0], az_r.at[0]), both(r2, ax_s.at[0], ax_r.at[0]),
         both(r1, ac_s.at[0], ac_r.at[0]),
     ])
 
-    for k in ORDER:
-        stage_x(k)
-
-    for k in ORDER:
+    weight(0)
+    weight(1)
+    stage_x(0)
+    stage_x(1)
+    arrived(1)
+    weight(2)
+    weight(3)
+    mx[...] += nt(w_ref[:, HW:], gall[:, HW:])
+    stat2 = all_stats(
+        st2, jnp.sum(gt[...] * gain_col * mx[...], axis=0, keepdims=True), st2_s, st2_r
+    )
+    stage_x(2)
+    stage_x(3)
+    for k in (0, 1, 3, 2):
         stage_z(k)
+    gather_z(0)
+    gather_z(1)
     slope = sum_stats(st2, stat2) / INNER
     mixed = mx[...]
     gated = gt[...]
@@ -326,7 +372,7 @@
         for s0, t0 in ((0, 0), (128, 128)):
             dm = tn(xtb[c0:c0 + HD, s0:s0 + 128], dyb[:, t0:])
             qs[s0:s0 + 128, t0:] = (dm * ks[h, s0:s0 + 128, t0:].astype(F32)).astype(BF16)
-            ws[s0:s0 + 128, t0:] += dm * hs[h, s0:s0 + 128, t0:].astype(F32)
+            ws[s0:s0 + 128, t0:] += dm * hs[h, s0:s0 + 128, t0:]
         top = jnp.sum(nn(qs[0:128, :], tge[...]) * strict[0:128, :], axis=0, keepdims=True)
         low = jnp.sum(
             nn(qs[128:, 128:], tge[128:, 128:]) * strict[128:, 128:], axis=0, keepdims=True
@@ -351,6 +397,14 @@
     wb = ws[...].astype(BF16)
     dbc[:, 0:N] = nn(wb, call).astype(BF16)
     dbc[:, N:2 * N] = tn(wb, ball).astype(BF16)
+    ones = jnp.ones((8, T), F32)
+    pk[...] = jnp.zeros_like(pk)
+    pk[0:1, :] = ng[0:1, 0:128]
+    pk[1:2, :] = ng[0:1, 128:256]
+    for q in range(3):
+        pk[2 + q:3 + q, 0:NH] = nt(ones, pr[4 * q:4 * q + 4, :], HI)[0:1, :]
+    pc = send(pk, p1, p_s.at[0], p_r.at[0], (other_core, me))
+
     for o in far:
         send(
             dbc.at[rows((me + o) % NT, 16), :], dbr.at[o - 1],
@@ -358,47 +412,40 @@
         )
     d_all = both(dbr, db_s.at[0], db_r.at[0])
     sent.append(d_all)
-
-    ones = jnp.ones((8, T), F32)
-    pk[...] = jnp.zeros_like(pk)
-    pk[0:1, :] = ng[0:1, 0:128]
-    pk[1:2, :] = ng[0:1, 128:256]
-    for q in range(3):
-        pk[2 + q:3 + q, 0:NH] = nt(ones, pr[4 * q:4 * q + 4, :], HI)[0:1, :]
-    pc = send(pk, p1, p_s.at[0], p_r.at[0], (other_core, me))
-
-    for k in ORDER:
-        gather_z(k)
+    gather_z(3)
+    gather_z(2)
     pc.wait_recv()
     p2[xi] = pk[...] + p1[...]
     for o in (1, 2, 3):
         send(p2.at[xi], p2.at[xi], p_s.at[1], p_r.at[1], (at_x(o), me))
     px = both(p2.at[0:3], p_s.at[1], p_r.at[1])
+    gather_x(0)
+    gather_x(1)
     gx_ref[...] = dxt[...].T.astype(BF16)
-    for k in ORDER:
-        gather_x(k)
     px.wait_recv()
     p3[zl] = p2[0] + p2[1] + p2[2] + p2[3]
     for o in (1, 2, 3):
         send(p3.at[zl], p3.at[zl], p_s.at[2], p_r.at[2], (at_z(o), me))
     pz = both(p3.at[0:3], p_s.at[2], p_r.at[2])
     sent.extend([pc, px, pz])
+    gather_core(0)
+    gather_core(1)
+    gather_core(3)
+    gather_core(2)
+    pz.wait_recv()
+    tot = p3[0] + p3[1] + p3[2] + p3[3]
+    gn_ref[...] = tot[0:2, :]
+    gsk_ref[...] = tot[2, 0:NH]
+    gal_ref[...] = tot[3, 0:NH]
+    gdb_ref[...] = tot[4, 0:NH]
+    for k in range(CHUNKS):
+        gather_end(k)
     d_all.wait_recv()
     tot = dbc[rows(me, 16), :].astype(F32)
     for o in range(NT - 1):
         tot = tot + dbr[o].astype(F32)
     gb_ref[...] = tot[:, 0:N]
     gc_ref[...] = tot[:, N:2 * N]
-    for k in ORDER:
-        gather_core(k)
-    pz.wait_recv()
-    tot = p3[0] + p3[1] + p3[2] + p3[3]
-    gn_ref[...] = tot[0:2, :]
-    gsk_ref[...] = tot[2, 0:NH]
-    gal_ref[...] = tot[3, 0:NH]
-    gdb_ref[...] = tot[4, 0:NH]
-    for k in ORDER:
-        gather_end(k)
     for copy in sent:
         copy.wait_send()
 
@@ -419,7 +466,7 @@
     scratch = [
         v((T, 2 * N), BF16), v((T, DW), BF16), v((NT, 2, 128), F32), v((NT, 2, 128), F32),
         v((CHUNKS, C, CW), BF16), v((CHUNKS, 128, CW), BF16), v((CHUNKS, 128, CW), BF16),
-        v((CHUNKS, 3, 32, CW), BF16), v((CHUNKS, 4, 32, 128), BF16), v((CHUNKS, 3, 32, 128), BF16),
+        v((CHUNKS, 3, 32, CW), BF16), v((CHUNKS, 4, 32, 128), BF16), v((CHUNKS, 4, 32, CW), BF16), v((CHUNKS, 3, 32, 128), BF16),
         v((T, 2 * N), BF16), v((peers, 16, 2 * N), BF16),
         v((8, 128), F32), v((8, 128), F32), v((4, 8, 128), F32), v((4, 8, 128), F32),
         v((T, C), BF16), v((T, C), BF16), v((NH, T), F32), pltpu.SMEM((NH,), F32),
@@ -427,11 +474,11 @@
         v((1, T), jnp.int32),
         v((16, T), F32), v((16, T), F32), v((T, T), F32), v((T, T), BF16),
         v((C, T), F32), v((C, T), BF16), v((C, T), F32), v((C, T), F32), v((C, T), F32),
-        v((C, T), F32), v((NH, T, T), BF16), v((NH, T, T), BF16), v((T, T), BF16),
+        v((C, T), F32), v((NH, T, T), BF16), v((NH, T, T), F32), v((T, T), BF16),
         v((T, T), F32), v((C, T), F32), v((C, T), BF16), v((C, T), F32),
         dma((12,)),
     ]
-    counts = [(1, 1), (1, 17), (1, 1), (1, 1)] + [(1, CHUNKS)] * 6 + [(1, 1), (3, 3)]
+    counts = [(1, 1), (2, 30), (1, 1), (1, 1)] + [(1, CHUNKS)] * 2 + [(CHUNKS, CHUNKS)] + [(1, CHUNKS)] * 3 + [(1, 1), (3, 3)]
     for n in counts:
         scratch += [dma((n[0],)), dma((n[1],))]
     out = jax.ShapeDtypeStruct

time: 66.1 us -> 64.3 us (0.973)
  Pallas kernels: 65.3 us -> 62.9 us
    pallas_call x1, Pallas kernels: 62.8 us -> 60.4 us  [per_device(): pl.pallas_call(kernel, out_shape=(out((T, C), BF16), out((T, C), BF16), o...]
where the time goes in v3:
time: 64.3 us; the launch traced here: 63.5 us
  Pallas kernels  62.9 us (98%)
  between operations  0.66 us (1%)
    pallas_call x1, Pallas kernels, per_device(): pl.pallas_call(kernel, out_shape=(out((T, C), BF16), out((T, C), BF16), o...  60.4 us
    pallas_call x1, Pallas kernels, per_device(): pl.pallas_call(finish, out_shape=tuple((out(r.shape, r.dtype) for r in re...  2.46 us

profile of v3, /device:TPU:1, one launch (start us, length us, event | category | flops | bytes accessed | tf_op | source)
XLA Modules:
  0.0 63.5 jit_solution(11654895300066005260)
XLA Ops:
  0.6 60.4 %shard_map.195 = (bf16[256,256]{1,0:T(8,128)(2,1)}, bf16[256,256]{1,0:T(8,128)(2,1)}, f32[4,256]{1,0:T(4,128)}, f32[16,128]{1,0:T(8,128)}, f32[16,128]{1,0:T(8,1...) custom-call(bf16[256,256]{1,0:T(8,128)(2,1)} %x_hbm.1, ...), custom_call_target="tpu_custom_call" | custom-call | flops 2000000000 | bytes 4194304 | tf_op jit(solution)/shard_map/pallas_call | solution.py:488
  61.1 2.5 %shard_map.196 = (bf16[256,256]{1,0:T(8,128)(2,1)}, bf16[256,256]{1,0:T(8,128)(2,1)}, f32[4,256]{1,0:T(4,128)}, f32[16,128]{1,0:T(8,128)}, f32[16,128]{1,0:T(8,1...) custom-call(bf16[256,256]{1,0:T(8,128)(2,1)} %get-tuple-element.30.refs_0_, ...), custom_call_target="tpu_custom_call" | custom-call | tf_op jit(solution)/shard_map/pallas_call | solution.py:504

commit v4 on v3

--- a/solution.py
+++ b/solution.py
@@ -42,7 +42,7 @@
 def kernel(
     x_hbm, z_hbm, dt_hbm, b_hbm, c_hbm, al_hbm, sk_hbm, db_hbm, gain_hbm, w_hbm, g_hbm, ids_hbm,
     gx_ref, gz_ref, gdt_ref, gb_ref, gc_ref, gw_ref, gn_ref, gal_ref, gsk_ref, gdb_ref,
-    bc, gall, st1, st2, wk, r1, s2, r2, s3, s4, r3, dbc, dbr, pk, p1, p2, p3,
+    bc, gall, st1, st2, wk, r1, s2, r2, s3, s4, r3, dbc, dbr, dbp, dbq, pk, p1, p2, p3,
     x_ref, z_ref, dt_ref, al_ref, sk_ref, db_ref, gain_ref, w_ref, ids_ref,
     rw, pr, mb, tge, xt, xtb, silt, dst, yt, gt, ks, hs, qs, ws, dxt, nrm, mx,
     in_s, bc_s, bc_r, g_s, g_r, st1_s, st1_r, st2_s, st2_r, c_s, c_r, x_s, x_r, z_s, z_r,
@@ -62,8 +62,9 @@
     other_core = zl * 8 + xi * 2 + (1 - core)
     dp_peers = [other_core] + [at_x(o) for o in (1, 2, 3)] + [at_z(o) for o in (1, 2, 3)]
 
+    far = sorted(range(1, NT), key=lambda o: -min(o // 2, NY - o // 2))
     barrier = pltpu.get_barrier_semaphore()
-    for o in range(1, NT):
+    for o in far:
         pl.semaphore_signal(barrier, inc=1, device_id=(dp, (me + o) % NT), device_id_type=MESH)
     for peer in dp_peers:
         pl.semaphore_signal(barrier, inc=1, device_id=(peer, me), device_id_type=MESH)
@@ -111,14 +112,14 @@
         return gall.at[rows(slot, 16), part * HW:(part + 1) * HW]
 
     def push(part, kind, slot, hop, span):
-        i = part * 15 + 1 + kind * 7 + spans[kind].index(span)
+        i = part * 6 + (2 + kind * 2 + (span > 0) if abs(span) == 2 else 1)
         to = ((y + hop + NY) % NY) * 2 + zh
         mine = piece(slot, part)
         g_copies[part, kind, span] = send(mine, mine, g_s.at[part], g_r.at[i], (dp, to))
 
     def cross(part):
         mine = piece(me, part)
-        z_copies[part] = send(mine, mine, g_s.at[part], g_r.at[part * 15], (dp, partner))
+        z_copies[part] = send(mine, mine, g_s.at[part], g_r.at[part * 6], (dp, partner))
 
     def direct(part, kind):
         if kind:
@@ -136,12 +137,10 @@
             push(part, kind, slot, d, 3 * d)
 
     def arrived(part):
-        for (p, _, span), copy in g_copies.items():
-            if p == part and abs(span) != 2:
-                copy.wait_recv()
+        rest = gall.at[0:10 * 16, part * HW:(part + 1) * HW]
+        both(rest, g_s.at[part], g_r.at[part * 6 + 1]).wait_recv()
 
     cross(0)
-    far = sorted(range(1, NT), key=lambda o: -min(o // 2, NY - o // 2))
     for o in far:
         mine = bc.at[rows(me, 16), :]
         send(mine, mine, bc_s.at[0], bc_r.at[0], (dp, (me + o) % NT))
@@ -151,7 +150,7 @@
     direct(0, 0)
     cross(1)
     for part in (0, 1):
-        sent.append(both(gall.at[0:(NT - 1) * 16, 0:HW], g_s.at[part], g_r.at[part * 15]))
+        sent.append(both(gall.at[0:(NT - 1) * 16, 0:HW], g_s.at[part], g_r.at[part * 6]))
 
     for load in loads[3:9]:
         load.wait()
@@ -394,9 +393,6 @@
     pr[4:8, :] = dld * ld
     pr[8:12, :] = ddt
 
-    wb = ws[...].astype(BF16)
-    dbc[:, 0:N] = nn(wb, call).astype(BF16)
-    dbc[:, N:2 * N] = tn(wb, ball).astype(BF16)
     ones = jnp.ones((8, T), F32)
     pk[...] = jnp.zeros_like(pk)
     pk[0:1, :] = ng[0:1, 0:128]
@@ -405,20 +401,21 @@
         pk[2 + q:3 + q, 0:NH] = nt(ones, pr[4 * q:4 * q + 4, :], HI)[0:1, :]
     pc = send(pk, p1, p_s.at[0], p_r.at[0], (other_core, me))
 
-    for o in far:
-        send(
-            dbc.at[rows((me + o) % NT, 16), :], dbr.at[o - 1],
-            db_s.at[0], db_r.at[0], (dp, (me + o) % NT),
-        )
+    wb = ws[...].astype(BF16)
+    dbc[:, 0:N] = nn(wb, call).astype(BF16)
+    dbc[:, N:2 * N] = tn(wb, ball).astype(BF16)
+    for d in (4, 3, 5, 2, 6, 1, 7):
+        to = (y + d) % NY
+        send(dbc.at[rows(to, 32), :], dbr.at[d - 1], db_s.at[0], db_r.at[0], (dp, to * 2 + zh))
     d_all = both(dbr, db_s.at[0], db_r.at[0])
     sent.append(d_all)
-    gather_z(3)
-    gather_z(2)
     pc.wait_recv()
     p2[xi] = pk[...] + p1[...]
     for o in (1, 2, 3):
         send(p2.at[xi], p2.at[xi], p_s.at[1], p_r.at[1], (at_x(o), me))
     px = both(p2.at[0:3], p_s.at[1], p_r.at[1])
+    gather_z(3)
+    gather_z(2)
     gather_x(0)
     gather_x(1)
     gx_ref[...] = dxt[...].T.astype(BF16)
@@ -428,6 +425,14 @@
         send(p3.at[zl], p3.at[zl], p_s.at[2], p_r.at[2], (at_z(o), me))
     pz = both(p3.at[0:3], p_s.at[2], p_r.at[2])
     sent.extend([pc, px, pz])
+    d_all.wait_recv()
+    tot = dbc[rows(y, 32), :].astype(F32)
+    for o in range(NY - 1):
+        tot = tot + dbr[o].astype(F32)
+    dbp[0] = tot[0:16, :]
+    dbp[1] = tot[16:32, :]
+    d_last = send(dbp.at[1 - zh], dbq, db_s.at[1], db_r.at[1], (dp, partner))
+    sent.append(d_last)
     gather_core(0)
     gather_core(1)
     gather_core(3)
@@ -440,10 +445,8 @@
     gdb_ref[...] = tot[4, 0:NH]
     for k in range(CHUNKS):
         gather_end(k)
-    d_all.wait_recv()
-    tot = dbc[rows(me, 16), :].astype(F32)
-    for o in range(NT - 1):
-        tot = tot + dbr[o].astype(F32)
+    d_last.wait_recv()
+    tot = dbp[zh] + dbq[...]
     gb_ref[...] = tot[:, 0:N]
     gc_ref[...] = tot[:, N:2 * N]
     for copy in sent:
@@ -462,12 +465,12 @@
 def per_device(x, z, dt, b, c, a_log, skip, bias, gain, w, g, ids):
     v = pltpu.VMEM
     dma = pltpu.SemaphoreType.DMA
-    peers = NT - 1
     scratch = [
         v((T, 2 * N), BF16), v((T, DW), BF16), v((NT, 2, 128), F32), v((NT, 2, 128), F32),
         v((CHUNKS, C, CW), BF16), v((CHUNKS, 128, CW), BF16), v((CHUNKS, 128, CW), BF16),
         v((CHUNKS, 3, 32, CW), BF16), v((CHUNKS, 4, 32, 128), BF16), v((CHUNKS, 4, 32, CW), BF16), v((CHUNKS, 3, 32, 128), BF16),
-        v((T, 2 * N), BF16), v((peers, 16, 2 * N), BF16),
+        v((T, 2 * N), BF16), v((NY - 1, 32, 2 * N), BF16), v((2, 16, 2 * N), F32),
+        v((16, 2 * N), F32),
         v((8, 128), F32), v((8, 128), F32), v((4, 8, 128), F32), v((4, 8, 128), F32),
         v((T, C), BF16), v((T, C), BF16), v((NH, T), F32), pltpu.SMEM((NH,), F32),
         pltpu.SMEM((NH,), F32), pltpu.SMEM((NH,), F32), v((1, C), F32), v((C, DW), BF16),
@@ -478,7 +481,7 @@
         v((T, T), F32), v((C, T), F32), v((C, T), BF16), v((C, T), F32),
         dma((12,)),
     ]
-    counts = [(1, 1), (2, 30), (1, 1), (1, 1)] + [(1, CHUNKS)] * 2 + [(CHUNKS, CHUNKS)] + [(1, CHUNKS)] * 3 + [(1, 1), (3, 3)]
+    counts = [(1, 1), (2, 12), (1, 1), (1, 1)] + [(1, CHUNKS)] * 2 + [(CHUNKS, CHUNKS)] + [(1, CHUNKS)] * 3 + [(2, 2), (3, 3)]
     for n in counts:
         scratch += [dma((n[0],)), dma((n[1],))]
     out = jax.ShapeDtypeStruct

time: 64.3 us -> 64.3 us (level)
  no operation moved by 1% of the time
where the time goes in v4:
time: 64.3 us; the launch traced here: 64.1 us
  Pallas kernels  63.4 us (99%)
  between operations  0.66 us (1%)
    pallas_call x1, Pallas kernels, per_device(): pl.pallas_call(kernel, out_shape=(out((T, C), BF16), out((T, C), BF16), o...  61 us
    pallas_call x1, Pallas kernels, per_device(): pl.pallas_call(finish, out_shape=tuple((out(r.shape, r.dtype) for r in re...  2.46 us

profile of v4, /device:TPU:1, one launch (start us, length us, event | category | flops | bytes accessed | tf_op | source)
XLA Modules:
  0.0 64.1 jit_solution(6274174346503877849)
XLA Ops:
  0.6 61.0 %shard_map.195 = (bf16[256,256]{1,0:T(8,128)(2,1)}, bf16[256,256]{1,0:T(8,128)(2,1)}, f32[4,256]{1,0:T(4,128)}, f32[16,128]{1,0:T(8,128)}, f32[16,128]{1,0:T(8,1...) custom-call(bf16[256,256]{1,0:T(8,128)(2,1)} %x_hbm.1, ...), custom_call_target="tpu_custom_call" | custom-call | flops 2000000000 | bytes 4194304 | tf_op jit(solution)/shard_map/pallas_call | solution.py:491
  61.6 2.5 %shard_map.196 = (bf16[256,256]{1,0:T(8,128)(2,1)}, bf16[256,256]{1,0:T(8,128)(2,1)}, f32[4,256]{1,0:T(4,128)}, f32[16,128]{1,0:T(8,128)}, f32[16,128]{1,0:T(8,1...) custom-call(bf16[256,256]{1,0:T(8,128)(2,1)} %get-tuple-element.30.refs_0_, ...), custom_call_target="tpu_custom_call" | custom-call | tf_op jit(solution)/shard_map/pallas_call | solution.py:507

commit v5 on v4

--- a/solution.py
+++ b/solution.py
@@ -348,8 +348,6 @@
     stage_x(3)
     for k in (0, 1, 3, 2):
         stage_z(k)
-    gather_z(0)
-    gather_z(1)
     slope = sum_stats(st2, stat2) / INNER
     mixed = mx[...]
     gated = gt[...]
@@ -387,6 +385,8 @@
     for h in range(NH):
         back(h)
 
+    gather_z(0)
+    gather_z(1)
     dld = pr[4:8, :]
     ddt = (pr[8:12, :] - ea * dld) * sig
     gdt_ref[...] = ddt
@@ -433,22 +433,22 @@
     dbp[1] = tot[16:32, :]
     d_last = send(dbp.at[1 - zh], dbq, db_s.at[1], db_r.at[1], (dp, partner))
     sent.append(d_last)
+    gather_core(3)
+    gather_core(2)
     gather_core(0)
     gather_core(1)
-    gather_core(3)
-    gather_core(2)
     pz.wait_recv()
     tot = p3[0] + p3[1] + p3[2] + p3[3]
     gn_ref[...] = tot[0:2, :]
     gsk_ref[...] = tot[2, 0:NH]
     gal_ref[...] = tot[3, 0:NH]
     gdb_ref[...] = tot[4, 0:NH]
-    for k in range(CHUNKS):
-        gather_end(k)
     d_last.wait_recv()
     tot = dbp[zh] + dbq[...]
     gb_ref[...] = tot[:, 0:N]
     gc_ref[...] = tot[:, N:2 * N]
+    for k in range(CHUNKS):
+        gather_end(k)
     for copy in sent:
         copy.wait_send()
 

time: 64.3 us -> 64.5 us (level)
  no operation moved by 1% of the time
where the time goes in v5:
time: 64.5 us; the launch traced here: 64.3 us
  Pallas kernels  63.6 us (99%)
  between operations  0.66 us (1%)
    pallas_call x1, Pallas kernels, per_device(): pl.pallas_call(kernel, out_shape=(out((T, C), BF16), out((T, C), BF16), o...  61.2 us
    pallas_call x1, Pallas kernels, per_device(): pl.pallas_call(finish, out_shape=tuple((out(r.shape, r.dtype) for r in re...  2.46 us

profile of v5, /device:TPU:1, one launch (start us, length us, event | category | flops | bytes accessed | tf_op | source)
XLA Modules:
  0.0 64.3 jit_solution(340536418707319131)
XLA Ops:
  0.6 61.2 %shard_map.195 = (bf16[256,256]{1,0:T(8,128)(2,1)}, bf16[256,256]{1,0:T(8,128)(2,1)}, f32[4,256]{1,0:T(4,128)}, f32[16,128]{1,0:T(8,128)}, f32[16,128]{1,0:T(8,1...) custom-call(bf16[256,256]{1,0:T(8,128)(2,1)} %x_hbm.1, ...), custom_call_target="tpu_custom_call" | custom-call | flops 2000000000 | bytes 4194304 | tf_op jit(solution)/shard_map/pallas_call | solution.py:491
  61.8 2.5 %shard_map.196 = (bf16[256,256]{1,0:T(8,128)(2,1)}, bf16[256,256]{1,0:T(8,128)(2,1)}, f32[4,256]{1,0:T(4,128)}, f32[16,128]{1,0:T(8,128)}, f32[16,128]{1,0:T(8,1...) custom-call(bf16[256,256]{1,0:T(8,128)(2,1)} %get-tuple-element.30.refs_0_, ...), custom_call_target="tpu_custom_call" | custom-call | tf_op jit(solution)/shard_map/pallas_call | solution.py:507

commit v6 on v5

--- a/solution.py
+++ b/solution.py
@@ -203,7 +203,6 @@
 
     direct(0, 1)
     forward(0, 0)
-    direct(1, 0)
     bc_all.wait_recv()
     ball = bc[:, 0:N]
     call = bc[:, N:2 * N]
@@ -236,6 +235,7 @@
     gated = gt[...]
     stat1 = all_stats(st1, jnp.sum(gated * gated, axis=0, keepdims=True), st1_s, st1_r)
 
+    direct(1, 0)
     forward(0, 1)
     direct(1, 1)
     forward(1, 0)

time: 64.5 us -> 64.6 us (level)
  no operation moved by 1% of the time
where the time goes in v6:
time: 64.6 us; the launch traced here: 64.4 us
  Pallas kernels  63.7 us (99%)
  between operations  0.66 us (1%)
    pallas_call x1, Pallas kernels, per_device(): pl.pallas_call(kernel, out_shape=(out((T, C), BF16), out((T, C), BF16), o...  61.3 us
    pallas_call x1, Pallas kernels, per_device(): pl.pallas_call(finish, out_shape=tuple((out(r.shape, r.dtype) for r in re...  2.46 us

profile of v6, /device:TPU:1, one launch (start us, length us, event | category | flops | bytes accessed | tf_op | source)
XLA Modules:
  0.0 64.4 jit_solution(1068188229801545750)
XLA Ops:
  0.6 61.3 %shard_map.195 = (bf16[256,256]{1,0:T(8,128)(2,1)}, bf16[256,256]{1,0:T(8,128)(2,1)}, f32[4,256]{1,0:T(4,128)}, f32[16,128]{1,0:T(8,128)}, f32[16,128]{1,0:T(8,1...) custom-call(bf16[256,256]{1,0:T(8,128)(2,1)} %x_hbm.1, ...), custom_call_target="tpu_custom_call" | custom-call | flops 2000000000 | bytes 4194304 | tf_op jit(solution)/shard_map/pallas_call | solution.py:491
  61.9 2.5 %shard_map.196 = (bf16[256,256]{1,0:T(8,128)(2,1)}, bf16[256,256]{1,0:T(8,128)(2,1)}, f32[4,256]{1,0:T(4,128)}, f32[16,128]{1,0:T(8,128)}, f32[16,128]{1,0:T(8,1...) custom-call(bf16[256,256]{1,0:T(8,128)(2,1)} %get-tuple-element.30.refs_0_, ...), custom_call_target="tpu_custom_call" | custom-call | tf_op jit(solution)/shard_map/pallas_call | solution.py:507
